TPU v7x, 32 devices: a whole 2x2x4 slice. The times are simulated.
32 devices in a mesh: shard: 2 (over core), context: 4 (over y, x), tensor: 4 (over z).
Axes of the slice: x: 2, y: 2, z: 4, core: 2. Of those that a mesh axis runs over, the one named last changes fastest.
Arguments:
- tokens: bfloat16 [16384, 1024], P(('shard', 'context', 'tensor')), may hold values from -6 to 6
- segments: int32 [8, 2048], P(('shard', 'tensor')), may hold values from 0 to 4, as said below
- attention_gain: float32 [1024], replicated, may hold values from 0.25 to 1.75
- query_weight: bfloat16 [1024, 1024], P(('shard', 'context'), 'tensor'), may hold values from -0.1875 to 0.1875
- key_weight: bfloat16 [1024, 512], P(('shard', 'context'), 'tensor'), may hold values from -0.1875 to 0.1875
- value_weight: bfloat16 [1024, 512], P(('shard', 'context'), 'tensor'), may hold values from -0.1875 to 0.1875
- query_gain: float32 [64], replicated, may hold values from 0.25 to 1.75
- key_gain: float32 [64], replicated, may hold values from 0.25 to 1.75
- output_weight: bfloat16 [1024, 1024], P(('shard', 'context'), 'tensor'), may hold values from -0.75 to 0.75
- feedforward_gain: float32 [1024], replicated, may hold values from 0.25 to 1.75
- gate_weight: bfloat16 [1024, 4608], P(('shard', 'context'), 'tensor'), may hold values from -0.1875 to 0.1875
- up_weight: bfloat16 [1024, 4608], P(('shard', 'context'), 'tensor'), may hold values from -0.1875 to 0.1875
- down_weight: bfloat16 [1024, 4608], P(('shard', 'context'), 'tensor'), may hold values from -0.125 to 0.125
- cotangent: bfloat16 [16384, 1024], P(('shard', 'context', 'tensor')), may hold values from -6 to 6
Outputs:
- block_output: float32 [16384, 1024], P(('shard', 'context', 'tensor'))
- token_grad: float32 [16384, 1024], P(('shard', 'context', 'tensor'))
- attention_gain_grad: float32 [1024], replicated
- query_weight_grad: float32 [1024, 1024], P(('shard', 'context'), 'tensor')
- key_weight_grad: float32 [1024, 512], P(('shard', 'context'), 'tensor')
- value_weight_grad: float32 [1024, 512], P(('shard', 'context'), 'tensor')
- query_gain_grad: float32 [64], replicated
- key_gain_grad: float32 [64], replicated
- output_weight_grad: float32 [1024, 1024], P(('shard', 'context'), 'tensor')
- feedforward_gain_grad: float32 [1024], replicated
- gate_weight_grad: float32 [1024, 4608], P(('shard', 'context'), 'tensor')
- up_weight_grad: float32 [1024, 4608], P(('shard', 'context'), 'tensor')
- down_weight_grad: float32 [1024, 4608], P(('shard', 'context'), 'tensor')
Inputs may be any that keep to these rules, and one draw needn't show every extreme that they name: `segments`: in each group's row the document numbers start at 0, never fall and rise by at most one from one token to the next; every group holds the same number of documents; each document holds 1 to 1024 tokens, and exactly one document of each group holds 1024.
All inputs are finite; a program needn't handle non-finite values.
Results may differ from a plain program's by a relative error of at most 0.017.
Values may be sent and summed in bfloat16 or wider, within the bound.
A program may use at most 192 MiB of HBM per device.

v0:
```python
import jax
import jax.numpy as jnp
from jax import lax
from jax.sharding import PartitionSpec as P

QHEADS = 16
KVHEADS = 8
HEAD = 64
BLK = 128


epsilon = 1e-05
rope_base = 1000000.0
contract_rows = (((0,), (0,)), ((), ()))
contract_cols = (((1,), (1,)), ((), ()))


def rms_norm(values, gain_vec):
    return (
        values * lax.rsqrt(jnp.mean(values * values, axis=-1, keepdims=True) + epsilon) * gain_vec
    )


def rotate(values, cosine, sine_table):
    half_dim = values.shape[-1] // 2
    turned = jnp.concatenate([-values[..., half_dim:], values[..., :half_dim]], axis=-1)
    return values * cosine + turned * sine_table


def tables(segment_row):
    length = segment_row.shape[0]
    places = jnp.arange(length, dtype=jnp.int32)
    seg_start = jnp.concatenate(
        [jnp.ones((1,), dtype=jnp.bool_), segment_row[1:] != segment_row[:-1]]
    )
    starts = lax.cummax(jnp.where(seg_start, places, jnp.zeros_like(places)), axis=0)
    position = (places - starts).astype(jnp.float32)
    frequency = rope_base ** (-2.0 * jnp.arange(HEAD // 2, dtype=jnp.float32) / HEAD)
    angles = position[:, None] * frequency[None, :]
    angles = jnp.concatenate([angles, angles], axis=1)
    return (position, jnp.cos(angles), jnp.sin(angles))


def product(left, right):
    return jnp.dot(left, right, preferred_element_type=jnp.float32)


def product_cols(left, right):
    return lax.dot_general(left, right, contract_cols, preferred_element_type=jnp.float32)


def product_rows(left, right):
    return lax.dot_general(left, right, contract_rows, preferred_element_type=jnp.float32)


def silu_parts(gate_pre):
    logistic = jax.nn.sigmoid(gate_pre)
    return (gate_pre * logistic, logistic * (1.0 + gate_pre * (1.0 - logistic)))


def on_device(
    tokens,
    segments,
    attention_gain,
    query_weight,
    key_weight,
    value_weight,
    query_gain,
    key_gain,
    output_weight,
    feedforward_gain,
    gate_weight,
    up_weight,
    down_weight,
    cotangent,
):
    context_size = lax.axis_size("context")
    tok_rows = tokens.shape[0]
    group_rows = segments.shape[1]
    layout_blocks = tok_rows // BLK
    query_width = QHEADS * HEAD
    kv_width = KVHEADS * HEAD
    local_queries = QHEADS // context_size
    local_kv = KVHEADS // context_size
    head_ratio = QHEADS // KVHEADS
    query_cols = query_width // context_size
    kv_cols = kv_width // context_size
    block_rows = min(512, group_rows)
    block_count = group_rows // block_rows
    score_scale = HEAD ** (-0.5)
    bfloat = jnp.bfloat16
    row_pieces = (
        lax.all_gather(query_weight, ("shard", "context"), axis=0, tiled=True),
        lax.all_gather(key_weight, ("shard", "context"), axis=0, tiled=True),
        lax.all_gather(value_weight, ("shard", "context"), axis=0, tiled=True),
        lax.all_gather(output_weight, ("shard", "context"), axis=0, tiled=True),
        lax.all_gather(gate_weight, ("shard", "context"), axis=0, tiled=True),
        lax.all_gather(up_weight, ("shard", "context"), axis=0, tiled=True),
        lax.all_gather(down_weight, ("shard", "context"), axis=0, tiled=True),
    )
    query_full, key_full, value_full, output_full = (
        lax.all_gather(row_pieces[0], "tensor", axis=1, tiled=True),
        lax.all_gather(row_pieces[1], "tensor", axis=1, tiled=True),
        lax.all_gather(row_pieces[2], "tensor", axis=1, tiled=True),
        lax.all_gather(row_pieces[3], "tensor", axis=1, tiled=True),
    )
    gate_full = row_pieces[4]
    up_full = row_pieces[5]
    down_full = row_pieces[6]

    def to_arrival(values):
        shaped = values.reshape((layout_blocks, context_size, BLK) + values.shape[1:])
        return jnp.swapaxes(shaped, 0, 1).reshape(values.shape)

    pos_stream, cos_stream, sin_stream = tables(segments[0])
    seg_here = to_arrival(segments[0])
    pos_here = to_arrival(pos_stream)
    cos_here = to_arrival(cos_stream)
    sin_here = to_arrival(sin_stream)
    inputs_f32 = tokens.astype(jnp.float32)
    normed_f32, norm_in_pull = jax.vjp(rms_norm, inputs_f32, attention_gain)
    normed_in = normed_f32.astype(bfloat)
    query_tok = product(normed_in, query_full).astype(bfloat)
    key_tok = product(normed_in, key_full).astype(bfloat)
    value_tok = product(normed_in, value_full).astype(bfloat)
    query_send = query_tok.reshape(tok_rows, context_size, query_cols)
    kv_send = jnp.concatenate(
        [
            key_tok.reshape(tok_rows, context_size, kv_cols),
            value_tok.reshape(tok_rows, context_size, kv_cols),
        ],
        axis=2,
    )
    query_arrived, kv_arrived = (
        lax.all_to_all(query_send, "context", split_axis=1, concat_axis=0, tiled=True),
        lax.all_to_all(kv_send, "context", split_axis=1, concat_axis=0, tiled=True),
    )
    query_heads = query_arrived.reshape(group_rows, local_queries, HEAD).astype(jnp.float32)
    key_heads = kv_arrived[:, 0, :kv_cols].reshape(group_rows, local_kv, HEAD).astype(jnp.float32)
    value_heads = kv_arrived[:, 0, kv_cols:].reshape(group_rows, local_kv, HEAD)

    def rotate_both(query_raw, key_raw, gain_query, gain_key):
        query_out = rotate(
            rms_norm(query_raw, gain_query), cos_here[:, None, :], sin_here[:, None, :]
        )
        key_out = rotate(rms_norm(key_raw, gain_key), cos_here[:, None, :], sin_here[:, None, :])
        return (query_out, key_out)

    rotated, rotate_pull = jax.vjp(rotate_both, query_heads, key_heads, query_gain, key_gain)
    query_rot = rotated[0].astype(bfloat)
    key_rot = rotated[1].astype(bfloat)

    def scores_for(first_row):
        query_block = lax.dynamic_slice_in_dim(query_rot, first_row, block_rows, 0)
        grouped = query_block.reshape(block_rows, local_kv, head_ratio, HEAD)
        raw_scores = (
            jnp.einsum("bgrh,kgh->grbk", grouped, key_rot, preferred_element_type=jnp.float32)
            * score_scale
        )
        seg_block = lax.dynamic_slice_in_dim(seg_here, first_row, block_rows, 0)
        pos_block = lax.dynamic_slice_in_dim(pos_here, first_row, block_rows, 0)
        allowed = (seg_block[:, None] == seg_here[None, :]) & (
            pos_here[None, :] <= pos_block[:, None]
        )
        return (jnp.where(allowed[None, None], raw_scores, -1e30), grouped)

    def forward_block(first_row):
        scores, _ = scores_for(first_row)
        row_max = jnp.max(scores, axis=-1, keepdims=True)
        lifted = jnp.exp(scores - row_max)
        row_total = jnp.sum(lifted, axis=-1, keepdims=True)
        weights = (lifted / row_total).astype(bfloat)
        mixture = jnp.einsum(
            "grbk,kgh->bgrh", weights, value_heads, preferred_element_type=jnp.float32
        )
        return (
            mixture.reshape(block_rows, local_queries * HEAD).astype(bfloat),
            (row_max + jnp.log(row_total))[..., 0],
        )

    block_starts = jnp.arange(block_count, dtype=jnp.int32) * block_rows
    attended_blocks, logsum_blocks = lax.map(forward_block, block_starts)
    attended_heads = attended_blocks.reshape(group_rows, 1, local_queries * HEAD)
    attended_back = lax.all_to_all(
        attended_heads, "context", split_axis=0, concat_axis=1, tiled=True
    )
    attended = attended_back.reshape(tok_rows, query_width)
    hidden_in = inputs_f32 + product_cols(attended, output_full)
    mid_f32, mid_pull = jax.vjp(rms_norm, hidden_in, feedforward_gain)
    normed_mid = mid_f32.astype(bfloat)
    normed_rows, grad_rows = (
        lax.all_gather(normed_mid, "tensor", axis=0, tiled=True),
        lax.all_gather(cotangent, "tensor", axis=0, tiled=True),
    )
    gate_pre = product(normed_rows, gate_full)
    up_pre = product(normed_rows, up_full)
    silu_gate, silu_slope = silu_parts(gate_pre)
    activated = (silu_gate * up_pre).astype(bfloat)
    ffn_output = lax.psum_scatter(
        product_cols(activated, down_full).astype(jnp.bfloat16),
        "tensor",
        scatter_dimension=0,
        tiled=True,
    ).astype(jnp.float32)
    d_activated = product(grad_rows, down_full)
    d_gate = (d_activated * up_pre * silu_slope).astype(bfloat)
    d_up = (d_activated * silu_gate).astype(bfloat)
    down_grad = product_rows(grad_rows, activated)
    gate_grad = product_rows(normed_rows, d_gate)
    up_grad = product_rows(normed_rows, d_up)
    d_normed_mid = lax.psum_scatter(
        product_cols(d_gate, gate_full) + product_cols(d_up, up_full),
        "tensor",
        scatter_dimension=0,
        tiled=True,
    )
    block_output = hidden_in + ffn_output
    d_hidden_mid, feedforward_gain_grad = mid_pull(d_normed_mid)
    d_hidden = cotangent.astype(jnp.float32) + d_hidden_mid
    d_branch = d_hidden.astype(bfloat)
    output_grad = product_rows(d_branch, attended)
    d_attended_tok = product(d_branch, output_full).astype(bfloat)
    d_attended = lax.all_to_all(
        d_attended_tok.reshape(tok_rows, context_size, query_cols),
        "context",
        split_axis=1,
        concat_axis=0,
        tiled=True,
    )
    d_attended = d_attended.reshape(group_rows, local_queries * HEAD)

    def backward_block(carried, inputs):
        key_acc, value_acc = carried
        first_row, logsum = inputs
        scores, grouped = scores_for(first_row)
        probs = jnp.exp(scores - logsum[..., None])
        probs_low = probs.astype(bfloat)
        grad_block = lax.dynamic_slice_in_dim(d_attended, first_row, block_rows, 0).reshape(
            block_rows, local_kv, head_ratio, HEAD
        )
        d_probs = jnp.einsum(
            "bgrh,kgh->grbk", grad_block, value_heads, preferred_element_type=jnp.float32
        )
        row_dot = jnp.sum(probs * d_probs, axis=-1, keepdims=True)
        d_scores = (probs * (d_probs - row_dot)).astype(bfloat)
        d_query_block = (
            jnp.einsum("grbk,kgh->bgrh", d_scores, key_rot, preferred_element_type=jnp.float32)
            * score_scale
        )
        key_acc = (
            key_acc
            + jnp.einsum("grbk,bgrh->kgh", d_scores, grouped, preferred_element_type=jnp.float32)
            * score_scale
        )
        value_acc = value_acc + jnp.einsum(
            "grbk,bgrh->kgh", probs_low, grad_block, preferred_element_type=jnp.float32
        )
        return ((key_acc, value_acc), d_query_block.reshape(block_rows, local_queries, HEAD))

    zero_heads = jnp.zeros((group_rows, local_kv, HEAD), jnp.float32)
    (d_key_rot, d_value_heads), d_query_blocks = lax.scan(
        backward_block, (zero_heads, zero_heads), (block_starts, logsum_blocks)
    )
    d_query_rot = d_query_blocks.reshape(group_rows, local_queries, HEAD)
    d_query_heads, d_key_heads, query_gain_grad, key_gain_grad = rotate_pull(
        (d_query_rot, d_key_rot)
    )
    d_query_send = d_query_heads.reshape(group_rows, 1, query_cols).astype(bfloat)
    d_kv_send = jnp.concatenate(
        [
            d_key_heads.reshape(group_rows, 1, kv_cols),
            d_value_heads.reshape(group_rows, 1, kv_cols),
        ],
        axis=2,
    ).astype(bfloat)
    d_query_back, d_kv_back = (
        lax.all_to_all(d_query_send, "context", split_axis=0, concat_axis=1, tiled=True),
        lax.all_to_all(d_kv_send, "context", split_axis=0, concat_axis=1, tiled=True),
    )
    d_query = d_query_back.reshape(tok_rows, query_width)
    d_key = d_kv_back[:, :, :kv_cols].reshape(tok_rows, kv_width)
    d_value = d_kv_back[:, :, kv_cols:].reshape(tok_rows, kv_width)
    query_grad = product_rows(normed_in, d_query)
    key_grad = product_rows(normed_in, d_key)
    value_grad = product_rows(normed_in, d_value)
    d_normed_in = (
        product_cols(d_query, query_full)
        + product_cols(d_key, key_full)
        + product_cols(d_value, value_full)
    )
    d_inputs_norm, attention_gain_grad = norm_in_pull(d_normed_in)
    token_grad = d_hidden + d_inputs_norm
    query_sum, key_sum, value_sum, output_sum = (
        lax.psum_scatter(
            query_grad.astype(jnp.bfloat16), "tensor", scatter_dimension=1, tiled=True
        ).astype(jnp.float32),
        lax.psum_scatter(
            key_grad.astype(jnp.bfloat16), "tensor", scatter_dimension=1, tiled=True
        ).astype(jnp.float32),
        lax.psum_scatter(
            value_grad.astype(jnp.bfloat16), "tensor", scatter_dimension=1, tiled=True
        ).astype(jnp.float32),
        lax.psum_scatter(
            output_grad.astype(jnp.bfloat16), "tensor", scatter_dimension=1, tiled=True
        ).astype(jnp.float32),
    )
    query_owned, key_owned, value_owned, output_owned, gate_owned, up_owned, down_owned = (
        lax.psum_scatter(query_sum, ("shard", "context"), scatter_dimension=0, tiled=True),
        lax.psum_scatter(key_sum, ("shard", "context"), scatter_dimension=0, tiled=True),
        lax.psum_scatter(value_sum, ("shard", "context"), scatter_dimension=0, tiled=True),
        lax.psum_scatter(output_sum, ("shard", "context"), scatter_dimension=0, tiled=True),
        lax.psum_scatter(gate_grad, ("shard", "context"), scatter_dimension=0, tiled=True),
        lax.psum_scatter(up_grad, ("shard", "context"), scatter_dimension=0, tiled=True),
        lax.psum_scatter(down_grad, ("shard", "context"), scatter_dimension=0, tiled=True),
    )
    attention_gain_total, query_gain_total, key_gain_total, feedforward_gain_total = lax.psum(
        (attention_gain_grad, query_gain_grad, key_gain_grad, feedforward_gain_grad),
        ("shard", "context", "tensor"),
    )
    return (
        block_output,
        token_grad,
        attention_gain_total,
        query_owned,
        key_owned,
        value_owned,
        query_gain_total,
        key_gain_total,
        output_owned,
        feedforward_gain_total,
        gate_owned,
        up_owned,
        down_owned,
    )


def solution(mesh):
    placed = (
        P(("shard", "context", "tensor"), None),
        P(("shard", "tensor"), None),
        P(),
        P(("shard", "context"), "tensor"),
        P(("shard", "context"), "tensor"),
        P(("shard", "context"), "tensor"),
        P(),
        P(),
        P(("shard", "context"), "tensor"),
        P(),
        P(("shard", "context"), "tensor"),
        P(("shard", "context"), "tensor"),
        P(("shard", "context"), "tensor"),
        P(("shard", "context", "tensor"), None),
    )
    return jax.shard_map(
        on_device,
        mesh=mesh,
        in_specs=placed,
        out_specs=(
            P(("shard", "context", "tensor"), None),
            P(("shard", "context", "tensor"), None),
            P(),
            P(("shard", "context"), "tensor"),
            P(("shard", "context"), "tensor"),
            P(("shard", "context"), "tensor"),
            P(),
            P(),
            P(("shard", "context"), "tensor"),
            P(),
            P(("shard", "context"), "tensor"),
            P(("shard", "context"), "tensor"),
            P(("shard", "context"), "tensor"),
        ),
        check_vma=False,
    )
```

profile of v0, /device:TPU:0, one launch (start us, length us, event | category | flops | bytes accessed | tf_op | source)
XLA Modules:
  0.0 1541.5 jit_solution(4349756373909175970)
XLA Ops:
  7.2 27.7 %all_gather.43 = bf16[1024,128]{1,0:T(8,128)(2,1)} all-gather(bf16[128,128]{1,0:T(8,128)(2,1)} %param.23), channel_id=1, replica_groups=mesh['shard'=2,'context'=4,'tensor'=4] {'shard','context'}, dimensions={0}, use_global_device_ids=true | all-gather | bytes 294912 | tf_op jit(solution)/shard_map/all_gather | solution.py:95
  35.0 26.0 %all_gather.41 = bf16[1024,128]{1,0:T(8,128)(2,1)} all-gather(bf16[128,128]{1,0:T(8,128)(2,1)} %param.22), channel_id=1, replica_groups=mesh['shard'=2,'context'=4,'tensor'=4] {'shard','context'}, dimensions={0}, use_global_device_ids=true | all-gather | bytes 294912 | tf_op jit(solution)/shard_map/all_gather | solution.py:94
  61.1 27.0 %all_gather.39 = bf16[1024,256]{1,0:T(8,128)(2,1)} all-gather(bf16[128,256]{1,0:T(8,128)(2,1)} %param.21), channel_id=1, replica_groups=mesh['shard'=2,'context'=4,'tensor'=4] {'shard','context'}, dimensions={0}, use_global_device_ids=true | all-gather | bytes 589824 | tf_op jit(solution)/shard_map/all_gather | solution.py:93
  88.2 26.5 %all_gather.45 = bf16[1024,256]{1,0:T(8,128)(2,1)} all-gather(bf16[128,256]{1,0:T(8,128)(2,1)S(1)} %copy-done.47), channel_id=1, replica_groups=mesh['shard'=2,'context'=4,'tensor'=4] {'shard','context'}, dimensions={0}, use_global_device_ids=true | all-gather | bytes 589824 | tf_op jit(solution)/shard_map/all_gather | solution.py:96
  130.5 9.9 all-to-all-done.1
  155.1 11.9 all-to-all-done
  177.4 73.5 %while.27 = (s32[]{:T(128)}, bf16[4,512,256]{2,1,0:T(8,128)(2,1)}, f32[4,2,2,512]{3,2,1,0:T(2,128)}, s32[4]{0:T(128)S(1)}, s32[2048]{0:T(1024)S(1)}, /*index=5*/...) while((s32[]{:T(128)}, bf16[4,512,256]{2,1,0:T(8,128)(2,1)}, ...), condition=%wide.region_8.9_spmd, body=%wide.region_5.8_spmd.sunk | while | flops 1127348224 | bytes 57766096 | solution.py:182
  254.5 17.0 %all_to_all.90 = bf16[4,2,65536]{2,1,0:T(2,128)(2,1)} all-to-all(bf16[4,2,65536]{2,1,0:T(2,128)(2,1)S(1)} %reshape.484), channel_id=1, replica_groups=mesh['shard'=2,'context'=4,'tensor'=4] {'context'}, dimensions={0} | all-to-all | bytes 2097152 | tf_op jit(solution)/shard_map/all_to_all | solution.py:184
  284.7 78.2 %all-gather.18.cloned.1.call-done = bf16[2048,1024]{1,0:T(8,128)(2,1)} async-done(((bf16[512,1024]{1,0:T(8,128)(2,1)}), bf16[2048,1024]{1,0:T(8,128)(2,1)}) %all-gather.18.cloned.1.call-update) | async-done | bytes 4194320 | tf_op jit(solution)/shard_map/all_gather | solution.py:192
  362.8 10.2 fusion.67
  373.0 19.3 %all-gather.20.cloned.1.call-done = bf16[1024,1152]{1,0:T(8,128)(2,1)} async-done(((bf16[128,1152]{1,0:T(8,128)(2,1)}), bf16[1024,1152]{1,0:T(8,128)(2,1)}) %all-gather.20.cloned.1.call-update) | async-done | bytes 2359312 | tf_op jit(solution)/shard_map/all_gather | solution.py:97
  392.3 10.2 fusion.66
  402.5 20.7 %all-gather.24.cloned.1.call-done = bf16[1024,1152]{1,0:T(8,128)(2,1)} async-done(((bf16[128,1152]{1,0:T(8,128)(2,1)}), bf16[1024,1152]{1,0:T(8,128)(2,1)}) %all-gather.24.cloned.1.call-update) | async-done | bytes 2359312 | tf_op jit(solution)/shard_map/all_gather | solution.py:99
  423.2 82.4 %all-gather.26.cloned.1.call-done = bf16[2048,1024]{1,0:T(8,128)(2,1)} async-done(((bf16[512,1024]{1,0:T(8,128)(2,1)}), bf16[2048,1024]{1,0:T(8,128)(2,1)}) %all-gather.26.cloned.1.call-update) | async-done | bytes 4194320 | tf_op jit(solution)/shard_map/all_gather | solution.py:193
  505.6 17.4 %multiply_convert_fusion = (bf16[2048,1152]{1,0:T(8,128)(2,1)}, bf16[2048,1152]{1,0:T(8,128)(2,1)S(1)}, bf16[2048,1152]{1,0:T(8,128)(2,1)}) fusion(f32[2048,1152]{1,0:T(8,128)} %fusion.66, f32[2048,1152]{1,0:T(8,128)} %fusion.67, bf16[2048,1024]{1,0:T(8,128)(2,1)} %all-gather.26.cloned.1.call-done, bf16[1024,1152]{1,0:T(8,128)(2,1)} %all-gather.24.cloned.1.call-done), kind=kOutput, calls=%fused_computation.45 | convolution fusion | flops 4867227648 | bytes 39583744 | tf_op jit(solution)/shard_map/dot_general | solution.py:45
  529.0 8.4 convolution_add_fusion
  537.4 9.9 convolution_convert_fusion
  547.4 133.2 %reduce-scatter.20.cloned.1.call-done = f32[512,1024]{1,0:T(8,128)} async-done(((f32[2048,1024]{1,0:T(8,128)}), f32[512,1024]{1,0:T(8,128)}) %reduce-scatter.20.cloned.1.call-update) | async-done | bytes 2097168 | tf_op jit(solution)/shard_map/reduce_scatter | solution.py:211
  683.3 77.1 %reduce-scatter.18.cloned.1.call-done = bf16[512,1024]{1,0:T(8,128)(2,1)} async-done(((bf16[2048,1024]{1,0:T(8,128)(2,1)}), bf16[512,1024]{1,0:T(8,128)(2,1)}) %reduce-scatter.18.cloned.1.call-update) | async-done | bytes 1048592 | tf_op jit(solution)/shard_map/reduce_scatter | solution.py:199
  771.3 13.9 all-to-all-done.3
  785.3 244.7 %while.28 = (s32[]{:T(128)}, f32[2048,2,64]{0,2,1:T(8,128)}, f32[2048,2,64]{0,2,1:T(8,128)}, f32[4,512,4,64]{1,0,3,2:T(4,128)}, s32[4]{0:T(128)S(1)}, /*index=5*...) while((s32[]{:T(128)}, f32[2048,2,64]{0,2,1:T(8,128)}, ...), condition=%wide.region_15.16_spmd.clone, body=%wide.region_13.15_spmd.clone.sunk | while | flops 2751854592 | bytes 186405520 | solution.py:261
  802.2 11.0 fusion.147
  813.2 10.9 fusion.148
  833.5 11.1 dynamic_update_slice.20
  862.6 11.0 fusion.147
  873.6 10.9 fusion.148
  895.2 11.1 dynamic_update_slice.20
  917.3 7.0 fusion.150
  924.3 11.0 fusion.147
  935.3 10.9 fusion.148
  956.8 11.1 dynamic_update_slice.20
  985.9 11.0 fusion.147
  996.9 10.9 fusion.148
  1018.5 11.1 dynamic_update_slice.20
  1036.5 16.8 %all_to_all.91 = bf16[4,2,65536]{2,1,0:T(2,128)(2,1)} all-to-all(bf16[4,2,65536]{2,1,0:T(2,128)(2,1)S(1)} %reshape.488), channel_id=1, replica_groups=mesh['shard'=2,'context'=4,'tensor'=4] {'context'}, dimensions={0} | all-to-all | bytes 2097152 | tf_op jit(solution)/shard_map/all_to_all | solution.py:278
  1071.0 9.8 convolution_bitcast_fusion.1
  1089.7 14.6 all_to_all.92
  1110.8 10.3 fusion.72
  1121.2 10.7 fusion.71
  1136.2 24.7 %reduce-scatter.30.cloned.1.call-done = bf16[1024,256]{1,0:T(8,128)(2,1)} async-done(((bf16[1024,1024]{1,0:T(8,128)(2,1)}), bf16[1024,256]{1,0:T(8,128)(2,1)}) %reduce-scatter.30.cloned.1.call-update) | async-done | bytes 524304 | tf_op jit(solution)/shard_map/reduce_scatter | solution.py:303
  1163.3 54.1 %reduce-scatter.38.cloned.1.call-done = f32[128,1152]{0,1:T(8,128)} async-done(((f32[1024,1152]{0,1:T(8,128)}), f32[128,1152]{0,1:T(8,128)}) %reduce-scatter.38.cloned.1.call-update) | async-done | bytes 589840 | tf_op jit(solution)/shard_map/reduce_scatter | solution.py:314
  1219.5 44.0 %reduce-scatter.22.cloned.1.call-done = bf16[1024,256]{1,0:T(8,128)(2,1)} async-done(((bf16[1024,1024]{1,0:T(8,128)(2,1)}), bf16[1024,256]{1,0:T(8,128)(2,1)}) %reduce-scatter.22.cloned.1.call-update) | async-done | bytes 524304 | tf_op jit(solution)/shard_map/reduce_scatter | solution.py:294
  1270.3 39.8 %all-reduce.4 = (f32[1024]{0:T(1024)}, f32[64]{0:T(128)}, f32[64]{0:T(128)}, f32[1024]{0:T(1024)}) all-reduce(f32[1024]{0:T(1024)S(1)} %get-tuple-element.364, f32[64]{0:T(128)S(1)} %get-tuple-element.362, f32[64]{0:T(128)S(1)} %get-tuple-element.366, ...), channel_id=1, replica_groups=mesh['shard'=2,'context'=4,'tensor'=4] {'shard','context','tensor'}, use_global_device_ids=true, to_apply=%region_20.21 | all-reduce | flops 2176 | bytes 17408 | tf_op jit(solution)/shard_map/psum | solution.py:316
  1320.8 58.2 %reduce-scatter.34.cloned.1.call-done = f32[128,1152]{1,0:T(8,128)} async-done(((f32[1024,1152]{1,0:T(8,128)}), f32[128,1152]{1,0:T(8,128)}) %reduce-scatter.34.cloned.1.call-update) | async-done | bytes 589840 | tf_op jit(solution)/shard_map/reduce_scatter | solution.py:312
  1379.0 37.8 %reduce-scatter.26.cloned.1.call-done = f32[128,128]{1,0:T(8,128)} async-done(((f32[1024,128]{1,0:T(8,128)}), f32[128,128]{1,0:T(8,128)}) %reduce-scatter.26.cloned.1.call-update) | async-done | bytes 65552 | tf_op jit(solution)/shard_map/reduce_scatter | solution.py:309
  1416.8 38.0 %reduce-scatter.28.cloned.1.call-done = f32[128,128]{1,0:T(8,128)} async-done(((f32[1024,128]{1,0:T(8,128)}), f32[128,128]{1,0:T(8,128)}) %reduce-scatter.28.cloned.1.call-update) | async-done | bytes 65552 | tf_op jit(solution)/shard_map/reduce_scatter | solution.py:310
  1454.8 39.8 %reduce-scatter.32.cloned.1.call-done = f32[128,256]{1,0:T(8,128)} async-done(((f32[1024,256]{1,0:T(8,128)}), f32[128,256]{1,0:T(8,128)}) %reduce-scatter.32.cloned.1.call-update) | async-done | bytes 131088 | tf_op jit(solution)/shard_map/reduce_scatter | solution.py:311
  1494.6 39.8 %reduce-scatter.24.cloned.1.call-done = f32[128,256]{1,0:T(8,128)} async-done(((f32[1024,256]{1,0:T(8,128)}), f32[128,256]{1,0:T(8,128)}) %reduce-scatter.24.cloned.1.call-update) | async-done | bytes 131088 | tf_op jit(solution)/shard_map/reduce_scatter | solution.py:308
  (473 shorter events, 304.9 us)
Async XLA Ops:
  7.2 81.0 %copy-start.47 = (bf16[128,256]{1,0:T(8,128)(2,1)S(1)}, bf16[128,256]{1,0:T(8,128)(2,1)}, u32[]{:S(2)}) copy-start(bf16[128,256]{1,0:T(8,128)(2,1)} %param.26) | copy-start | bytes 196612
  7.2 108.1 %copy-start.19 = (bf16[512,1024]{1,0:T(8,128)(2,1)S(1)}, bf16[512,1024]{1,0:T(8,128)(2,1)}, u32[]{:S(2)}) copy-start(bf16[512,1024]{1,0:T(8,128)(2,1)} %param.18) | copy-start | bytes 3145732
  7.2 109.4 %all-gather.14.cloned.1.call-start = ((), (), s32[]{:S(2)}) async-start(), calls=%async_computation.21 | async-start | bytes 1310720 | tf_op jit(solution)/shard_map/all_gather | solution.py:104
  35.0 80.6 %copy-start.46 = (s32[1,2048]{1,0:T(1,128)S(1)}, s32[1,2048]{1,0:T(1,128)}, u32[]{:S(2)}) copy-start(s32[1,2048]{1,0:T(1,128)} %param.19) | copy-start | bytes 24580
  35.0 81.7 %copy-start.53 = (f32[1024]{0:T(1024)S(1)}, f32[1024]{0:T(1024)}, u32[]{:S(2)}) copy-start(f32[1024]{0:T(1024)} %param.20) | copy-start | bytes 12292
  35.0 84.0 %all-gather.12.cloned.1.call-start = ((), (), s32[]{:S(2)}) async-start(), calls=%async_computation.20 | async-start | bytes 1310720 | tf_op jit(solution)/shard_map/all_gather | solution.py:103
  61.1 83.5 %all-gather.10.cloned.1.call-start = ((), (), s32[]{:S(2)}) async-start(), calls=%async_computation.19 | async-start | bytes 2621440 | tf_op jit(solution)/shard_map/all_gather | solution.py:102
  88.1 189.4 %all-gather.16.cloned.1.call-start = ((), (), s32[]{:S(2)}) async-start(), calls=%async_computation.22 | async-start | bytes 2621440 | tf_op jit(solution)/shard_map/all_gather | solution.py:105
  114.7 170.0 %all-gather.22.cloned.1.call-start = ((), (), s32[]{:S(2)}) async-start(), calls=%async_computation.25 | async-start | bytes 2654208 | tf_op jit(solution)/shard_map/all_gather | solution.py:98
  115.6 29.0 %copy-start.49 = (f32[512]{0:T(512)}, f32[512]{0:T(512)S(1)}, u32[]{:S(2)}) copy-start(f32[512]{0:T(512)S(1)} %fusion.54) | copy-start | bytes 6148
  122.5 17.9 %all-to-all-start.1 = ((bf16[512,4,256]{2,0,1:T(8,128)(2,1)}), bf16[512,4,256]{2,0,1:T(8,128)(2,1)S(1)}, u32[]{:S(2)}, u32[]{:S(2)}) async-start(bf16[512,4,256]{2,0,1:T(8,128)(2,1)} %pad_maximum_fusion), calls=%async_computation.1 | async-start | bytes 2097152 | tf_op jit(solution)/shard_map/all_to_all | solution.py:136
  130.1 24.5 %copy-start.16 = (f32[2048,64]{0,1:T(8,128)}, f32[2048,64]{0,1:T(8,128)S(1)}, u32[]{:S(2)}) copy-start(f32[2048,64]{0,1:T(8,128)S(1)} %mul.369) | copy-start | bytes 1572868
  130.4 24.3 %copy-start.13 = (f32[2048,64]{0,1:T(8,128)}, f32[2048,64]{0,1:T(8,128)S(1)}, u32[]{:S(2)}) copy-start(f32[2048,64]{0,1:T(8,128)S(1)} %mul.372) | copy-start | bytes 1572868
  148.9 18.0 %all-to-all-start = ((bf16[512,4,256]{2,0,1:T(8,128)(2,1)}), bf16[512,4,256]{2,0,1:T(8,128)(2,1)}, u32[]{:S(2)}, u32[]{:S(2)}) async-start(bf16[512,4,256]{2,0,1:T(8,128)(2,1)} %bitcast.310), calls=%async_computation | async-start | bytes 2097152 | tf_op jit(solution)/shard_map/all_to_all | solution.py:135
  153.1 209.7 %all-gather.18.cloned.1.call-start = ((), (), s32[]{:S(2)}) async-start(), calls=%async_computation.23 | async-start | bytes 5242880 | tf_op jit(solution)/shard_map/all_gather | solution.py:192
  282.3 109.9 %all-gather.20.cloned.1.call-start = ((), (), s32[]{:S(2)}) async-start(), calls=%async_computation.24 | async-start | bytes 2654208 | tf_op jit(solution)/shard_map/all_gather | solution.py:97
  283.1 140.1 %all-gather.24.cloned.1.call-start = ((), (), s32[]{:S(2)}) async-start(), calls=%async_computation.26 | async-start | bytes 2654208 | tf_op jit(solution)/shard_map/all_gather | solution.py:99
  283.8 221.7 %all-gather.26.cloned.1.call-start = ((), (), s32[]{:S(2)}) async-start(), calls=%async_computation.28 | async-start | bytes 5242880 | tf_op jit(solution)/shard_map/all_gather | solution.py:193
  284.6 396.0 %reduce-scatter.20.cloned.1.call-start = ((), (), s32[]{:S(2)}) async-start(), calls=%async_computation.29 | async-start | bytes 10485760 | tf_op jit(solution)/shard_map/reduce_scatter | solution.py:211
  505.6 17.4 %copy-start.61 = (bf16[1024,1152]{1,0:T(8,128)(2,1)S(1)}, bf16[1024,1152]{1,0:T(8,128)(2,1)}, u32[]{:S(2)}) copy-start(bf16[1024,1152]{1,0:T(8,128)(2,1)} %all-gather.20.cloned.1.call-done) | copy-start | bytes 7077892
  537.4 223.0 %reduce-scatter.18.cloned.1.call-start = ((), (), s32[]{:S(2)}) async-start(), calls=%async_computation.27 | async-start | bytes 5242880 | tf_op jit(solution)/shard_map/reduce_scatter | solution.py:199
  767.0 18.3 %all-to-all-start.3 = ((bf16[512,4,256]{2,0,1:T(8,128)(2,1)}), bf16[512,4,256]{2,0,1:T(8,128)(2,1)}, u32[]{:S(2)}, u32[]{:S(2)}) async-start(bf16[512,4,256]{2,0,1:T(8,128)(2,1)} %bitcast.217), calls=%async_computation.5 | async-start | bytes 2097152 | tf_op jit(solution)/shard_map/all_to_all | solution.py:223
  771.3 360.7 %reduce-scatter.40.cloned.1.call-start = ((), (), s32[]{:S(2)}) async-start(), calls=%async_computation.39 | async-start | bytes 1310720
  832.9 11.7 copy-start.29
  833.0 11.7 copy-start.35
  833.0 11.7 copy-start.43
  894.6 11.7 copy-start.29
  894.6 11.7 copy-start.35
  894.6 11.7 copy-start.43
  956.3 11.7 copy-start.29
  956.3 11.7 copy-start.35
  956.3 11.7 copy-start.43
  1017.9 11.7 copy-start.29
  1017.9 11.7 copy-start.35
  1017.9 11.7 copy-start.43
  1061.6 72.5 %reduce-scatter.42.cloned.1.call-start = ((), (), s32[]{:S(2)}) async-start(), calls=%async_computation.40 | async-start | bytes 1310720
  1067.0 93.8 %reduce-scatter.30.cloned.1.call-start = ((), (), s32[]{:S(2)}) async-start(), calls=%async_computation.34 | async-start | bytes 2621440 | tf_op jit(solution)/shard_map/reduce_scatter | solution.py:303
  1071.0 146.4 %reduce-scatter.38.cloned.1.call-start = ((), (), s32[]{:S(2)}) async-start(), calls=%async_computation.38 | async-start | bytes 5308416 | tf_op jit(solution)/shard_map/reduce_scatter | solution.py:314
  1080.8 182.7 %reduce-scatter.22.cloned.1.call-start = ((), (), s32[]{:S(2)}) async-start(), calls=%async_computation.30 | async-start | bytes 2621440 | tf_op jit(solution)/shard_map/reduce_scatter | solution.py:294
  1110.7 210.1 %reduce-scatter.36.cloned.1.call-start = ((), (), s32[]{:S(2)}) async-start(), calls=%async_computation.37 | async-start | bytes 5308416 | tf_op jit(solution)/shard_map/reduce_scatter | solution.py:313
  1121.1 257.9 %reduce-scatter.34.cloned.1.call-start = ((), (), s32[]{:S(2)}) async-start(), calls=%async_computation.36 | async-start | bytes 5308416 | tf_op jit(solution)/shard_map/reduce_scatter | solution.py:312
  1131.9 284.8 %reduce-scatter.26.cloned.1.call-start = ((), (), s32[]{:S(2)}) async-start(), calls=%async_computation.32 | async-start | bytes 589824 | tf_op jit(solution)/shard_map/reduce_scatter | solution.py:309
  1134.0 320.8 %reduce-scatter.28.cloned.1.call-start = ((), (), s32[]{:S(2)}) async-start(), calls=%async_computation.33 | async-start | bytes 589824 | tf_op jit(solution)/shard_map/reduce_scatter | solution.py:310
  1136.1 358.5 %reduce-scatter.32.cloned.1.call-start = ((), (), s32[]{:S(2)}) async-start(), calls=%async_computation.35 | async-start | bytes 1179648 | tf_op jit(solution)/shard_map/reduce_scatter | solution.py:311
  1163.0 102.6 %copy-start.25 = (bf16[512,4,128]{0,2,1:T(8,128)(2,1)S(1)}, bf16[512,4,128]{0,2,1:T(8,128)(2,1)}, u32[]{:S(2)}) copy-start(bf16[512,4,128]{0,2,1:T(8,128)(2,1)} %copy-done.24) | copy-start | bytes 1572868
  1163.0 102.6 %copy-start.31 = (bf16[1024,512]{1,0:T(8,128)(2,1)S(1)}, bf16[1024,512]{1,0:T(8,128)(2,1)}, u32[]{:S(2)}) copy-start(bf16[1024,512]{1,0:T(8,128)(2,1)} %all-gather.12.cloned.1.call-done) | copy-start | bytes 3145732
  1163.0 371.4 %reduce-scatter.24.cloned.1.call-start = ((), (), s32[]{:S(2)}) async-start(), calls=%async_computation.31 | async-start | bytes 1179648 | tf_op jit(solution)/shard_map/reduce_scatter | solution.py:308
  1269.0 41.1 %copy-start.52 = (f32[512]{0:T(512)S(1)}, f32[512]{0:T(512)}, u32[]{:S(2)}) copy-start(f32[512]{0:T(512)} %copy-done.51) | copy-start | bytes 6148
  (85 other events, 396.2 us)
Sparse Core Ops, SparseCore 0:
  35.1 30.4 all-gather.13
  67.2 28.4 all-gather.11
  97.3 44.5 all-gather.9
  143.3 44.4 all-gather.15
  189.5 27.2 all-gather.21
  282.5 80.3 all-gather.17
  364.7 27.5 all-gather.19
  394.2 28.9 all-gather.23
  424.8 80.7 all-gather.25
  537.5 143.0 reduce-scatter.19
  682.8 77.4 reduce-scatter.17
  1061.7 26.1 reduce-scatter.39
  1090.2 25.8 reduce-scatter.41
  1118.3 42.4 reduce-scatter.29
  1164.2 53.1 reduce-scatter.37
  1219.7 43.8 reduce-scatter.21
  1267.4 53.3 reduce-scatter.35
  1325.1 53.8 reduce-scatter.33
  1382.7 34.0 reduce-scatter.25
  1420.6 34.1 reduce-scatter.27
  1458.5 36.0 reduce-scatter.31
  1498.4 36.0 reduce-scatter.23
where the time goes:
time: 1550 us; the launch traced here: 1540 us
  waiting for transfers between devices  793 us (51%)
  matrix products  274 us (18%)
  blocking collectives  195 us (13%)
  local copies, waits for them, and re-layouts  120 us (8%)
  other arithmetic  114 us (7%)
  loops' own time  17 us (1%)
  between operations  15.6 us (1%)
    reduce_scatter x1, waiting for transfers between devices, on_device(): lax.psum_scatter(product_cols(d_gate, gate_full) + product_cols(d_up, up_...  133 us
    all_gather x1, waiting for transfers between devices, on_device(): lax.all_gather(cotangent, 'tensor', axis=0, tiled=True)  82.4 us
    all_gather x1, waiting for transfers between devices, on_device(): lax.all_gather(normed_mid, 'tensor', axis=0, tiled=True)  78.2 us
    reduce_scatter x1, waiting for transfers between devices, on_device(): lax.psum_scatter(product_cols(activated, down_full).astype(jnp.bfloat16),...  77.1 us
    reduce_scatter x1, waiting for transfers between devices, on_device(): lax.psum_scatter(gate_grad, ('shard', 'context'), scatter_dimension=0, ti...  58.2 us
    reduce_scatter x1, waiting for transfers between devices, on_device(): lax.psum_scatter(down_grad, ('shard', 'context'), scatter_dimension=0, ti...  54.1 us
    dynamic_update_slice x8, local copies, waits for them, and re-layouts, on_device(): lax.scan(backward_block, (zero_heads, zero_heads), (block_starts, logsum_...  46.5 us
    dot_general x7, matrix products, product(): return jnp.dot(left, right, preferred_element_type=jnp.float32)  46.5 us
  transfers between devices with their start and end apart: 25, of which 18 were waited for; matrix products, arithmetic and copies ran while one was open for 14% of the time, Pallas kernels for 0%

commit v1 on v0

v1 whole, which is shorter than its diff:
```python
import jax
import jax.numpy as jnp
from jax import lax
from jax.experimental import pallas as pl
from jax.experimental.pallas import tpu as pltpu
from jax.sharding import PartitionSpec as P

QHEADS = 16
KVHEADS = 8
HEAD = 64
BLK = 128
MAXLEN = 1024
PAIR = 2 * HEAD


epsilon = 1e-05
rope_base = 1000000.0
contract_rows = (((0,), (0,)), ((), ()))
contract_cols = (((1,), (1,)), ((), ()))


def rms_norm(values, gain_vec):
    return (
        values * lax.rsqrt(jnp.mean(values * values, axis=-1, keepdims=True) + epsilon) * gain_vec
    )


def tables(segment_row):
    length = segment_row.shape[0]
    places = jnp.arange(length, dtype=jnp.int32)
    seg_start = jnp.concatenate(
        [jnp.ones((1,), dtype=jnp.bool_), segment_row[1:] != segment_row[:-1]]
    )
    starts = lax.cummax(jnp.where(seg_start, places, jnp.zeros_like(places)), axis=0)
    position = (places - starts).astype(jnp.float32)
    frequency = rope_base ** (-2.0 * jnp.arange(HEAD // 2, dtype=jnp.float32) / HEAD)
    angles = position[:, None] * frequency[None, :]
    cosine, sine = jnp.cos(angles), jnp.sin(angles)
    wide = PAIR // (HEAD // 2)
    return (
        starts[:, None],
        jnp.concatenate([cosine] * wide, axis=1),
        jnp.concatenate([sine] * wide, axis=1),
    )


def product(left, right):
    return jnp.dot(left, right, preferred_element_type=jnp.float32)


def product_cols(left, right):
    return lax.dot_general(left, right, contract_cols, preferred_element_type=jnp.float32)


def product_rows(left, right):
    return lax.dot_general(left, right, contract_rows, preferred_element_type=jnp.float32)


def silu_parts(gate_pre):
    logistic = jax.nn.sigmoid(gate_pre)
    return (gate_pre * logistic, logistic * (1.0 + gate_pre * (1.0 - logistic)))


def lane_half(rows):
    return lax.broadcasted_iota(jnp.int32, (rows, PAIR), 1) // HEAD


def half_mean(values, half):
    low_sum = jnp.sum(jnp.where(half == 0, values, 0.0), axis=1, keepdims=True)
    high_sum = jnp.sum(jnp.where(half == 0, 0.0, values), axis=1, keepdims=True)
    return jnp.where(half == 0, low_sum, high_sum) * (1.0 / HEAD)


def first_quarter(rows):
    lanes = lax.broadcasted_iota(jnp.int32, (rows, PAIR), 1)
    return lanes % HEAD < HEAD // 2


def norm_rope(values, gain, cosine, sine):
    rows = values.shape[0]
    inverse = lax.rsqrt(half_mean(values * values, lane_half(rows)) + epsilon)
    normed = values * inverse * gain
    turned = jnp.where(
        first_quarter(rows),
        -pltpu.roll(normed, PAIR - HEAD // 2, 1),
        pltpu.roll(normed, HEAD // 2, 1),
    )
    return normed * cosine + turned * sine


def norm_rope_back(grad, values, gain, cosine, sine):
    rows = values.shape[0]
    half = lane_half(rows)
    inverse = lax.rsqrt(half_mean(values * values, half) + epsilon)
    turned = jnp.where(
        first_quarter(rows),
        pltpu.roll(grad * sine, PAIR - HEAD // 2, 1),
        -pltpu.roll(grad * sine, HEAD // 2, 1),
    )
    d_normed = grad * cosine + turned
    gain_grad = jnp.sum(d_normed * values * inverse, axis=0, keepdims=True)
    scaled = d_normed * gain
    d_values = inverse * scaled - values * (inverse * inverse * inverse) * half_mean(
        scaled * values, half
    )
    return d_values, gain_grad


def twice(values, which):
    return jnp.where(lane_half(values.shape[0]) == which, values, pltpu.roll(values, HEAD, 1))


def stacked(values):
    half = lane_half(values.shape[0])
    return jnp.concatenate(
        [jnp.where(half == 0, values, 0.0), jnp.where(half == 0, 0.0, values)], axis=0
    ).astype(jnp.bfloat16)


def unstacked(values):
    half = lane_half(BLK)
    return jnp.where(half == 0, values[:BLK], values[BLK:])


def arrival(stream_block, contexts, blocks):
    return (stream_block % contexts) * blocks + stream_block // contexts


def prepare_keys(dims, k_ref, v_ref, cos_ref, sin_ref, kgain_ref, keys, values):
    contexts, blocks, _ = dims
    which = pl.program_id(0)

    @pl.when(pl.program_id(1) == 0)
    def _():
        def one(block, carried):
            source = pl.ds(pl.multiple_of(arrival(block, contexts, blocks) * BLK, BLK), BLK)
            target = pl.ds(pl.multiple_of(block * BLK, BLK), BLK)
            raw = twice(k_ref[source, :].astype(jnp.float32), which)
            keys[target, :] = norm_rope(
                raw, kgain_ref[...], cos_ref[target, :], sin_ref[target, :]
            ).astype(jnp.bfloat16)
            values[target, :] = twice(v_ref[source, :].astype(jnp.float32), which).astype(
                jnp.bfloat16
            )
            return carried

        lax.fori_loop(0, contexts * blocks, one, 0)


def block_probs(dims, q_ref, cos_ref, sin_ref, start_ref, qgain_ref, keys):
    window = dims[2]
    block = pl.program_id(1)
    here = pl.ds(pl.multiple_of(block * BLK, BLK), BLK)
    query_raw = q_ref[...].astype(jnp.float32)
    query = stacked(norm_rope(query_raw, qgain_ref[...], cos_ref[here, :], sin_ref[here, :]))
    first = pl.multiple_of(jnp.maximum(block * BLK + BLK - window, 0), BLK)
    span = pl.ds(first, window)
    scores = product_cols(query, keys[span, :]) * (HEAD ** (-0.5))
    shape = (BLK, window)
    column = lax.broadcasted_iota(jnp.int32, shape, 1) + first
    row = lax.broadcasted_iota(jnp.int32, shape, 0) + block * BLK
    allowed = (column >= start_ref[here, :]) & (column <= row)
    offset = jnp.where(allowed, 0.0, -1e30)
    scores = scores + jnp.concatenate([offset, offset], axis=0)
    lifted = jnp.exp(scores - jnp.max(scores, axis=1, keepdims=True))
    probs = lifted * (1.0 / jnp.sum(lifted, axis=1, keepdims=True))
    return query_raw, query, span, here, probs


def forward_kernel(
    dims, q_ref, k_ref, v_ref, cos_ref, sin_ref, start_ref, qgain_ref, kgain_ref, o_ref, keys, values
):
    prepare_keys(dims, k_ref, v_ref, cos_ref, sin_ref, kgain_ref, keys, values)
    _, _, span, _, probs = block_probs(
        dims, q_ref, cos_ref, sin_ref, start_ref, qgain_ref, keys
    )
    mixture = product(probs.astype(jnp.bfloat16), values[span, :])
    o_ref[...] = unstacked(mixture).astype(o_ref.dtype)


def backward_kernel(
    dims,
    q_ref,
    k_ref,
    v_ref,
    cos_ref,
    sin_ref,
    start_ref,
    qgain_ref,
    kgain_ref,
    d_ref,
    dq_ref,
    dk_ref,
    dv_ref,
    dqgain_ref,
    dkgain_ref,
    keys,
    values,
    key_acc,
    value_acc,
):
    contexts, blocks, _ = dims
    which = pl.program_id(0)
    block = pl.program_id(1)
    scale = HEAD ** (-0.5)
    prepare_keys(dims, k_ref, v_ref, cos_ref, sin_ref, kgain_ref, keys, values)

    @pl.when(block == 0)
    def _():
        key_acc[...] = jnp.zeros_like(key_acc)
        value_acc[...] = jnp.zeros_like(value_acc)

    @pl.when((block == 0) & (which == 0))
    def _():
        dqgain_ref[...] = jnp.zeros_like(dqgain_ref)
        dkgain_ref[...] = jnp.zeros_like(dkgain_ref)

    query_raw, query, span, here, probs = block_probs(
        dims, q_ref, cos_ref, sin_ref, start_ref, qgain_ref, keys
    )
    grad = stacked(d_ref[...].astype(jnp.float32))
    d_probs = product_cols(grad, values[span, :])
    row_dot = jnp.sum(probs * d_probs, axis=1, keepdims=True)
    d_scores = (probs * (d_probs - row_dot)).astype(jnp.bfloat16)
    value_acc[span, :] += product_rows(probs.astype(jnp.bfloat16), grad)
    key_acc[span, :] += product_rows(d_scores, query)
    d_query_rot = unstacked(product(d_scores, keys[span, :])) * scale
    d_query, gain_grad = norm_rope_back(
        d_query_rot, query_raw, qgain_ref[...], cos_ref[here, :], sin_ref[here, :]
    )
    dq_ref[...] = d_query.astype(dq_ref.dtype)
    dqgain_ref[0:1, :] += gain_grad

    @pl.when(block == contexts * blocks - 1)
    def _():
        half = lane_half(BLK)

        def one(item, carried):
            place = pl.ds(pl.multiple_of(arrival(item, contexts, blocks) * BLK, BLK), BLK)
            stream = pl.ds(pl.multiple_of(item * BLK, BLK), BLK)
            raw = twice(k_ref[place, :].astype(jnp.float32), which)
            d_key_rot = key_acc[stream, :]
            d_key_rot = (d_key_rot + pltpu.roll(d_key_rot, HEAD, 1)) * scale
            d_key, key_gain_grad = norm_rope_back(
                d_key_rot, raw, kgain_ref[...], cos_ref[stream, :], sin_ref[stream, :]
            )
            dkgain_ref[0:1, :] += key_gain_grad
            d_value = value_acc[stream, :]
            d_value = d_value + pltpu.roll(d_value, HEAD, 1)
            old_key = dk_ref[place, :].astype(jnp.float32)
            old_value = dv_ref[place, :].astype(jnp.float32)
            mine = half == which
            later = which > 0
            old_key = jnp.where(later, old_key, 0.0)
            old_value = jnp.where(later, old_value, 0.0)
            dk_ref[place, :] = jnp.where(mine, d_key, old_key).astype(dk_ref.dtype)
            dv_ref[place, :] = jnp.where(mine, d_value, old_value).astype(dv_ref.dtype)
            return carried

        lax.fori_loop(0, contexts * blocks, one, 0)


def attention(backward, contexts, qkv, cosine, sine, starts, gain_query, gain_key, d_attended):
    rows = qkv.shape[0]
    stream_blocks = rows // BLK
    blocks = stream_blocks // contexts
    window = min(MAXLEN + BLK, rows)
    pairs = QHEADS // contexts // 2
    dims = (contexts, blocks, window)

    def moving():
        return pl.BlockSpec((BLK, PAIR), lambda g, s: (arrival(s, contexts, blocks), g))

    def whole(shape, column=0):
        return pl.BlockSpec(shape, lambda g, s: (0, column))

    tall = (rows, PAIR)
    in_specs = [
        moving(),
        whole(tall, pairs),
        whole(tall, pairs + 1),
        whole(tall),
        whole(tall),
        whole((rows, 1)),
        whole((1, PAIR)),
        whole((1, PAIR)),
    ]
    operands = [
        qkv,
        qkv,
        qkv,
        cosine,
        sine,
        starts,
        jnp.concatenate([gain_query, gain_query])[None, :],
        jnp.concatenate([gain_key, gain_key])[None, :],
    ]
    scratch = [pltpu.VMEM(tall, jnp.bfloat16), pltpu.VMEM(tall, jnp.bfloat16)]
    params = pltpu.CompilerParams(
        dimension_semantics=("arbitrary", "arbitrary"), vmem_limit_bytes=48 * 1024 * 1024
    )
    products = 2 * 2 * stream_blocks * BLK * window * PAIR * pairs
    if not backward:
        return pl.pallas_call(
            lambda *refs: forward_kernel(dims, *refs),
            grid=(pairs, stream_blocks),
            in_specs=in_specs,
            out_specs=moving(),
            out_shape=jax.ShapeDtypeStruct((rows, pairs * PAIR), jnp.bfloat16),
            scratch_shapes=scratch,
            compiler_params=params,
            cost_estimate=pl.CostEstimate(
                flops=2 * products, bytes_accessed=10 * rows * PAIR * 4, transcendentals=0
            ),
            name="attention_forward",
        )(*operands)
    accs = [pltpu.VMEM(tall, jnp.float32), pltpu.VMEM(tall, jnp.float32)]
    return pl.pallas_call(
        lambda *refs: backward_kernel(dims, *refs),
        grid=(pairs, stream_blocks),
        in_specs=in_specs + [moving()],
        out_specs=[moving(), whole(tall), whole(tall), whole((8, PAIR)), whole((8, PAIR))],
        out_shape=[
            jax.ShapeDtypeStruct((rows, pairs * PAIR), jnp.bfloat16),
            jax.ShapeDtypeStruct(tall, jnp.bfloat16),
            jax.ShapeDtypeStruct(tall, jnp.bfloat16),
            jax.ShapeDtypeStruct((8, PAIR), jnp.float32),
            jax.ShapeDtypeStruct((8, PAIR), jnp.float32),
        ],
        scratch_shapes=scratch + accs,
        compiler_params=params,
        cost_estimate=pl.CostEstimate(
            flops=5 * products, bytes_accessed=16 * rows * PAIR * 4, transcendentals=0
        ),
        name="attention_backward",
    )(*operands, d_attended)


def on_device(
    tokens,
    segments,
    attention_gain,
    query_weight,
    key_weight,
    value_weight,
    query_gain,
    key_gain,
    output_weight,
    feedforward_gain,
    gate_weight,
    up_weight,
    down_weight,
    cotangent,
):
    contexts = lax.axis_size("context")
    tensors = lax.axis_size("tensor")
    tok_rows = tokens.shape[0]
    group_rows = segments.shape[1]
    hidden = gate_weight.shape[1]
    width = tokens.shape[1]
    query_cols = query_weight.shape[1]
    kv_cols = key_weight.shape[1]
    qkv_cols = query_cols + 2 * kv_cols
    rows_axes = ("shard", "context")
    bfloat = jnp.bfloat16

    def shift(values, step):
        pairs = [(i, (i + step) % tensors) for i in range(tensors)]
        return lax.ppermute(values, "tensor", pairs)

    attn_local = jnp.concatenate([query_weight, key_weight, value_weight, output_weight], axis=1)
    attn_cols = lax.all_gather(attn_local, "tensor", axis=0)
    qkv_weight = lax.all_gather(attn_cols[:, :, :qkv_cols], rows_axes, axis=1, tiled=True)
    grad_rows = [cotangent] + [shift(cotangent, step) for step in range(1, tensors)]

    starts, cosine, sine = tables(segments[0])
    inputs_f32 = tokens.astype(jnp.float32)
    normed_f32, norm_in_pull = jax.vjp(rms_norm, inputs_f32, attention_gain)
    normed_in = normed_f32.astype(bfloat)

    qkv_weight, out_local, gate_local, up_local, down_local = lax.optimization_barrier(
        (qkv_weight, attn_cols[:, :, qkv_cols:], gate_weight, up_weight, down_weight)
    )
    out_weight = lax.all_gather(out_local, rows_axes, axis=1, tiled=True)
    pair_weight = lax.all_gather(
        jnp.concatenate([gate_local, up_local], axis=1), rows_axes, axis=0, tiled=True
    )
    down_full = lax.all_gather(down_local, rows_axes, axis=0, tiled=True)

    qkv_send = jnp.einsum(
        "md,tdn->tmn", normed_in, qkv_weight, preferred_element_type=jnp.float32
    ).astype(bfloat)
    qkv = lax.all_to_all(qkv_send, "context", split_axis=0, concat_axis=0, tiled=True)
    qkv = qkv.reshape(group_rows, qkv_cols)
    mixed = attention(
        False, contexts, qkv, cosine, sine, starts, query_gain, key_gain, None
    )
    attended = lax.all_to_all(
        mixed.reshape(contexts, tok_rows, query_cols),
        "context",
        split_axis=0,
        concat_axis=0,
        tiled=True,
    )
    hidden_in = inputs_f32 + jnp.einsum(
        "tmk,tdk->md", attended, out_weight, preferred_element_type=jnp.float32
    )
    mid_f32, mid_pull = jax.vjp(rms_norm, hidden_in, feedforward_gain)
    normed_mid = mid_f32.astype(bfloat)
    normed_rows = [normed_mid] + [shift(normed_mid, step) for step in range(1, tensors)]

    outputs_part, grads_part = [], []
    pair_grad = down_grad = None
    for step in range(tensors):
        pre = product(normed_rows[step], pair_weight)
        d_activated = product(grad_rows[step], down_full)
        gate_pre, up_pre = pre[:, :hidden], pre[:, hidden:]
        silu_gate, silu_slope = silu_parts(gate_pre)
        activated = (silu_gate * up_pre).astype(bfloat)
        d_gate = (d_activated * up_pre * silu_slope).astype(bfloat)
        d_up = (d_activated * silu_gate).astype(bfloat)
        d_pair = jnp.concatenate([d_gate, d_up], axis=1)
        d_mid = product_cols(d_pair, pair_weight)
        if step > 0:
            d_mid = shift(d_mid.astype(bfloat), -step).astype(jnp.float32)
        grads_part.append(d_mid)
        outputs_part.append(product_cols(activated, down_full))
        pair_term = product_rows(normed_rows[step], d_pair)
        down_term = product_rows(grad_rows[step], activated)
        pair_grad = pair_term if step == 0 else pair_grad + pair_term
        down_grad = down_term if step == 0 else down_grad + down_term
    pair_owned = lax.psum_scatter(
        pair_grad.astype(bfloat), rows_axes, scatter_dimension=0, tiled=True
    )
    down_owned = lax.psum_scatter(
        down_grad.astype(bfloat), rows_axes, scatter_dimension=0, tiled=True
    )
    d_normed_mid = sum(grads_part[1:], grads_part[0])
    d_normed_mid, *late = lax.optimization_barrier(
        (d_normed_mid, *[part.astype(bfloat) for part in outputs_part[1:]])
    )
    ffn_output = outputs_part[0]
    for step in range(1, tensors):
        ffn_output = ffn_output + shift(late[step - 1], -step).astype(jnp.float32)
    block_output = hidden_in + ffn_output

    d_hidden_mid, feedforward_gain_grad = mid_pull(d_normed_mid)
    d_hidden = cotangent.astype(jnp.float32) + d_hidden_mid
    d_branch = d_hidden.astype(bfloat)
    d_attended_send = jnp.einsum(
        "md,tdk->tmk", d_branch, out_weight, preferred_element_type=jnp.float32
    ).astype(bfloat)
    d_attended = lax.all_to_all(
        d_attended_send, "context", split_axis=0, concat_axis=0, tiled=True
    ).reshape(group_rows, query_cols)
    out_grad = jnp.einsum(
        "md,tmk->tdk", d_branch, attended, preferred_element_type=jnp.float32
    ).astype(bfloat)
    out_rows = lax.psum_scatter(out_grad, rows_axes, scatter_dimension=1, tiled=True)

    d_query_here, d_key_here, d_value_here, query_gain_rows, key_gain_rows = attention(
        True, contexts, qkv, cosine, sine, starts, query_gain, key_gain, d_attended
    )
    query_gain_grad = query_gain_rows[0, :HEAD] + query_gain_rows[0, HEAD:]
    key_gain_grad = key_gain_rows[0, :HEAD]
    d_qkv_send = jnp.concatenate([d_query_here, d_key_here, d_value_here], axis=1)
    d_qkv = lax.all_to_all(
        d_qkv_send.reshape(contexts, tok_rows, qkv_cols),
        "context",
        split_axis=0,
        concat_axis=0,
        tiled=True,
    )
    qkv_grad = jnp.einsum(
        "md,tmn->tdn", normed_in, d_qkv, preferred_element_type=jnp.float32
    ).astype(bfloat)
    qkv_grad, pair_owned, down_owned, out_rows = lax.optimization_barrier(
        (qkv_grad, pair_owned, down_owned, out_rows)
    )
    qkv_rows = lax.psum_scatter(qkv_grad, rows_axes, scatter_dimension=1, tiled=True)
    d_normed_in = jnp.einsum(
        "tmn,tdn->md", d_qkv, qkv_weight, preferred_element_type=jnp.float32
    )
    d_inputs_norm, attention_gain_grad = norm_in_pull(d_normed_in)
    token_grad = d_hidden + d_inputs_norm
    attn_owned = lax.psum_scatter(
        jnp.concatenate([qkv_rows, out_rows], axis=2), "tensor", scatter_dimension=0, tiled=True
    )[0].astype(jnp.float32)
    gains = jnp.concatenate(
        [attention_gain_grad, feedforward_gain_grad, query_gain_grad, key_gain_grad]
    )
    gains = lax.all_gather(gains[None, :], ("shard", "context", "tensor"), axis=0, tiled=True)
    gains = jnp.sum(gains, axis=0)
    pair_owned = pair_owned.astype(jnp.float32)
    return (
        block_output,
        token_grad,
        gains[:width],
        attn_owned[:, :query_cols],
        attn_owned[:, query_cols : query_cols + kv_cols],
        attn_owned[:, query_cols + kv_cols : qkv_cols],
        gains[2 * width : 2 * width + HEAD],
        gains[2 * width + HEAD :],
        attn_owned[:, qkv_cols:],
        gains[width : 2 * width],
        pair_owned[:, :hidden],
        pair_owned[:, hidden:],
        down_owned.astype(jnp.float32),
    )


def solution(mesh):
    placed = (
        P(("shard", "context", "tensor"), None),
        P(("shard", "tensor"), None),
        P(),
        P(("shard", "context"), "tensor"),
        P(("shard", "context"), "tensor"),
        P(("shard", "context"), "tensor"),
        P(),
        P(),
        P(("shard", "context"), "tensor"),
        P(),
        P(("shard", "context"), "tensor"),
        P(("shard", "context"), "tensor"),
        P(("shard", "context"), "tensor"),
        P(("shard", "context", "tensor"), None),
    )
    return jax.shard_map(
        on_device,
        mesh=mesh,
        in_specs=placed,
        out_specs=(
            P(("shard", "context", "tensor"), None),
            P(("shard", "context", "tensor"), None),
            P(),
            P(("shard", "context"), "tensor"),
            P(("shard", "context"), "tensor"),
            P(("shard", "context"), "tensor"),
            P(),
            P(),
            P(("shard", "context"), "tensor"),
            P(),
            P(("shard", "context"), "tensor"),
            P(("shard", "context"), "tensor"),
            P(("shard", "context"), "tensor"),
        ),
        check_vma=False,
    )
```

time: 1550 us -> 911 us (0.59)
  waiting for transfers between devices: 793 us -> 253 us
  matrix products: 274 us -> 138 us
  Pallas kernels: 0 us -> 127 us
  starting transfers between devices: 13.3 us -> 135 us
  other arithmetic: 114 us -> 28.6 us
  local copies, waits for them, and re-layouts: 120 us -> 54.7 us
  blocking collectives: 195 us -> 151 us
  loops' own time: 17 us -> 0 us
    reduce_scatter x11 -> x2, waiting for transfers between devices: 554 us -> 19.7 us  [the longest x1 19.7 us: on_device(): lax.psum_scatter(jnp.concatenate([qkv_rows, out_rows], axis=2), 'tensor',...]
    all_gather x9 -> x4, waiting for transfers between devices: 201 us -> 35.5 us  [the longest x1 35.5 us: on_device(): lax.all_gather(attn_cols[:, :, :qkv_cols], rows_axes, axis=1, tiled=True)]
    ppermute x0 -> x12, waiting for transfers between devices: none -> 157 us  [shift(): return lax.ppermute(values, 'tensor', pairs)]
    dot_general x28 -> x6, matrix products: 155 us -> 26.2 us  [the longest x1 6.02 us: on_device(): jnp.einsum('tmn,tdn->md', d_qkv, qkv_weight, preferred_element_type=jnp.f...]
    pallas_call x0 -> x2, Pallas kernels: none -> 127 us  [the longest x1 81.2 us: attention(): pl.pallas_call(lambda *refs: backward_kernel(dims, *refs), grid=(pairs, s...]
    ppermute x0 -> x12, starting transfers between devices: none -> 126 us  [shift(): return lax.ppermute(values, 'tensor', pairs)]
    convert_element_type x13 -> x1, other arithmetic: 54.8 us -> 0.95 us  [on_device(): attn_owned = lax.psum_scatter(jnp.concatenate([qkv_rows, out_rows], axis=...]
    dynamic_update_slice x16 -> x0, local copies, waits for them, and re-layouts: 49.9 us -> none  [the longest x8 46.5 us: on_device(): lax.scan(backward_block, (zero_heads, zero_heads), (block_starts, logsum_...]
  transfers between devices with their start and end apart: 25 -> 23, of which waited for: 18 -> 10; matrix products, arithmetic and copies ran while one was open for 14% -> 21% of each run, Pallas kernels for 0% -> 14%
where the time goes in v1:
time: 911 us; the launch traced here: 902 us
  waiting for transfers between devices  253 us (28%)
  blocking collectives  151 us (17%)
  matrix products  138 us (15%)
  starting transfers between devices  135 us (15%)
  Pallas kernels  127 us (14%)
  local copies, waits for them, and re-layouts  54.7 us (6%)
  other arithmetic  28.6 us (3%)
  between operations  15 us (2%)
    ppermute x12, waiting for transfers between devices, shift(): return lax.ppermute(values, 'tensor', pairs)  157 us
    ppermute x12, starting transfers between devices, shift(): return lax.ppermute(values, 'tensor', pairs)  126 us
    all_gather x1, blocking collectives, on_device(): lax.all_gather(gains[None, :], ('shard', 'context', 'tensor'), axis=0, ti...  89.2 us
    pallas_call x1, Pallas kernels, attention(): pl.pallas_call(lambda *refs: backward_kernel(dims, *refs), grid=(pairs, s...  81.2 us
    dot_general x8, matrix products, product_rows(): lax.dot_general(left, right, contract_rows, preferred_element_type=jnp.fl...  50.7 us
    pallas_call x1, Pallas kernels, attention(): pl.pallas_call(lambda *refs: forward_kernel(dims, *refs), grid=(pairs, st...  45.9 us
    unnamed x104, local copies, waits for them, and re-layouts  39.8 us
    dot_general x8, matrix products, product(): return jnp.dot(left, right, preferred_element_type=jnp.float32)  36.4 us
  transfers between devices with their start and end apart: 23, of which 10 were waited for; matrix products, arithmetic and copies ran while one was open for 21% of the time, Pallas kernels for 14%

profile of v1, /device:TPU:0, one launch (start us, length us, event | category | flops | bytes accessed | tf_op | source)
XLA Modules:
  0.0 902.3 jit_solution(5558050895249097302)
XLA Ops:
  8.2 21.4 %all-gather = bf16[512,768]{1,0:T(8,128)(2,1)S(1)} all-gather(bf16[128,768]{1,0:T(8,128)(2,1)S(1)} %pad_maximum_fusion.27), channel_id=2, replica_groups=mesh['shard'=2,'context'=4,'tensor'=4] {'tensor'}, dimensions={0}, use_global_device_ids=true | all-gather | bytes 983040 | tf_op jit(solution)/shard_map/all_gather | solution.py:372
  31.3 35.5 %all-gather.8.cloned.1.call-done = bf16[4,1024,512]{2,1,0:T(8,128)(2,1)} async-done(((bf16[4,128,512]{2,1,0:T(8,128)(2,1)}), bf16[4,1024,512]{2,1,0:T(8,128)(2,1)}) %all-gather.8.cloned.1.call-update) | async-done | bytes 4194320 | tf_op jit(solution)/shard_map/all_gather | solution.py:373
  69.2 6.0 convert_bitcast_fusion.2
  75.2 4.6 all-to-all-start
  81.1 5.5 multiply_sine_fusion
  86.7 5.6 pad_maximum_fusion.23
  92.4 18.7 %all-to-all-done = bf16[4,512,512]{1,2,0:T(8,128)(2,1)} async-done(((bf16[4,512,512]{1,2,0:T(8,128)(2,1)}), bf16[4,512,512]{1,2,0:T(8,128)(2,1)}, u32[]{:S(2)}, u32[]{:S(2)}) %all-to-all-start) | async-done | bytes 2097184 | tf_op jit(solution)/shard_map/all_to_all | solution.py:393
  111.0 4.1 copy.60
  115.2 45.9 %attention_forward.1 = bf16[2048,256]{1,0:T(8,128)(2,1)S(1)} custom-call(bf16[2048,512]{1,0:T(8,128)(2,1)} %bitcast.127, bf16[2048,512]{1,0:T(8,128)(2,1)} %bitcast.128, bf16[2048,512]{1,0:T(8,128)(2,1)} %bitcast.129, f32[2048,128]{1,0:T(8,128)S(1)} %get-tuple-element.123.refs_3_, f32[2048,128]{1,0:T(8,128)S(1)} %get-tuple-element.124.refs_4_, ...), custom_call_target="tpu_custom_call" | custom-call | flops 4831838208 | bytes 10485760 | tf_op jit(solution)/shard_map/attention_forward/pallas_call | solution.py:304
  161.1 19.8 %all_to_all.20 = bf16[4,512,256]{2,1,0:T(8,128)(2,1)} all-to-all(bf16[4,512,256]{2,1,0:T(8,128)(2,1)S(1)} %bitcast.120), channel_id=1, replica_groups=mesh['shard'=2,'context'=4,'tensor'=4] {'context'}, dimensions={0} | all-to-all | bytes 2097152 | tf_op jit(solution)/shard_map/all_to_all | solution.py:398
  180.9 3.5 multiply_reduce_fusion.2
  195.3 19.1 %collective-permute-done.7 = bf16[512,1024]{1,0:T(8,128)(2,1)} collective-permute-done((bf16[512,1024]{1,0:T(8,128)(2,1)}, bf16[512,1024]{1,0:T(8,128)(2,1)}, u32[]{:S(2)}, u32[]{:S(2)}) %collective-permute-start.7) | collective-permute-done | bytes 1048608 | tf_op jit(solution)/shard_map/ppermute | solution.py:369
  215.1 7.5 fusion.52
  222.5 14.3 %collective-permute-done.6 = bf16[512,1024]{1,0:T(8,128)(2,1)} collective-permute-done((bf16[512,1024]{1,0:T(8,128)(2,1)}, bf16[512,1024]{1,0:T(8,128)(2,1)}, u32[]{:S(2)}, u32[]{:S(2)}) %collective-permute-start.6) | collective-permute-done | bytes 1048608 | tf_op jit(solution)/shard_map/ppermute | solution.py:369
  236.8 5.6 multiply_convert_fusion.4
  242.5 3.6 fusion.23
  246.1 112.9 %collective-permute-start.8 = (bf16[512,1024]{1,0:T(8,128)(2,1)}, bf16[512,1024]{1,0:T(8,128)(2,1)}, u32[]{:S(2)}, u32[]{:S(2)}) collective-permute-start(bf16[512,1024]{1,0:T(8,128)(2,1)} %fusion.23), channel_id=1, source_target_pairs={{0,1},{1,2},{2,3},{3,0},{4,5},{5,6},{6,7},{7,4},{8,9},{9,10},{10,1... | collective-permute-start | bytes 3145736 | tf_op jit(solution)/shard_map/ppermute | solution.py:369
  359.0 55.7 %collective-permute-done.4 = bf16[512,1024]{1,0:T(8,128)(2,1)} collective-permute-done((bf16[512,1024]{1,0:T(8,128)(2,1)}, bf16[512,1024]{1,0:T(8,128)(2,1)}, u32[]{:S(2)}, u32[]{:S(2)}) %collective-permute-start.4) | collective-permute-done | bytes 1048608 | tf_op jit(solution)/shard_map/ppermute | solution.py:369
  414.7 3.8 fusion.51
  422.0 3.6 fusion.22
  425.7 3.8 fusion.50
  429.5 3.4 multiply_convert_fusion.8
  433.0 3.7 fusion.21
  437.1 3.8 fusion.48
  441.0 4.9 multiply_convert_fusion.10
  454.4 4.3 fusion
  458.7 4.3 copy.84
  463.2 3.7 convolution_convert_fusion.3
  472.7 5.0 convert_add_fusion.1
  483.8 21.9 %collective-permute-done.11 = bf16[512,1024]{1,0:T(8,128)(2,1)S(1)} collective-permute-done((bf16[512,1024]{1,0:T(8,128)(2,1)S(1)}, bf16[512,1024]{1,0:T(8,128)(2,1)S(1)}, u32[]{:S(2)}, u32[]{:S(2)}) %collective-permute-start.11) | collective-permute-done | bytes 1048608 | tf_op jit(solution)/shard_map/ppermute | solution.py:369
  505.7 44.0 %collective-permute-done.10 = bf16[512,1024]{1,0:T(8,128)(2,1)S(1)} collective-permute-done((bf16[512,1024]{1,0:T(8,128)(2,1)S(1)}, bf16[512,1024]{1,0:T(8,128)(2,1)S(1)}, u32[]{:S(2)}, u32[]{:S(2)}) %collective-permute-start.10) | collective-permute-done | bytes 1048608 | tf_op jit(solution)/shard_map/ppermute | solution.py:369
  549.7 3.5 fusion.9
  557.3 4.3 copy.86
  565.3 8.4 fusion.19
  573.7 7.7 fusion.15
  581.4 7.7 fusion.17
  589.1 14.2 %add_convert_fusion = bf16[1024,2304]{1,0:T(8,128)(2,1)} fusion(f32[1024,2304]{1,0:T(8,128)} %fusion.15, f32[1024,2304]{1,0:T(8,128)} %fusion.19, f32[1024,2304]{1,0:T(8,128)} %fusion.17, bf16[512,1024]{1,0:T(8,128)(2,1)} %collective-permute-done.7, bf16[512,1152]{1,0:T(8,128)(2,1)S(1)} %copy-done.14, bf16[512,1152]{1,0:T(8,128)(2,1)S(1)} %copy-done.12), kind=kOutput, calls=%fused_computation | convolution fusion | flops 2430074880 | bytes 36438016 | tf_op jit(solution)/shard_map/dot_general | solution.py:56
  603.3 3.5 fusion.24
  606.8 20.8 %all_to_all.21 = bf16[4,512,256]{1,2,0:T(8,128)(2,1)} all-to-all(bf16[4,512,256]{1,2,0:T(8,128)(2,1)S(1)} %fusion.24), channel_id=1, replica_groups=mesh['shard'=2,'context'=4,'tensor'=4] {'context'}, dimensions={0} | all-to-all | bytes 2097152 | tf_op jit(solution)/shard_map/all_to_all | solution.py:453
  629.9 81.2 %attention_backward.1 = (bf16[2048,256]{1,0:T(8,128)(2,1)S(1)}, bf16[2048,128]{1,0:T(8,128)(2,1)S(1)}, bf16[2048,128]{1,0:T(8,128)(2,1)S(1)}, f32[8,128]{1,0:T(8,128)S(1)}, f32[8,128]{1,0:T(8,128)S(1)}) custom-call(bf16[2048,512]{1,0:T(8,128)(2,1)} %bitcast.130, bf16[2048,512]{1,0:T(8,128)(2,1)} %bitcast.131, bf16[2048,512]{1,0:T(8,128)(2,1)} %bitcast.132, ...), custom_call_target="tpu_custom_call" | custom-call | flops 12079595520 | bytes 16777216 | tf_op jit(solution)/shard_map/attention_backward/pallas_call | solution.py:318
  712.6 3.7 all-to-all-start.3
  717.6 21.3 %all-to-all-done.3 = bf16[4,512,512]{2,1,0:T(8,128)(2,1)S(1)} async-done(((bf16[4,512,512]{2,1,0:T(8,128)(2,1)}), bf16[4,512,512]{2,1,0:T(8,128)(2,1)S(1)}, u32[]{:S(2)}, u32[]{:S(2)}) %all-to-all-start.3) | async-done | bytes 2097184 | tf_op jit(solution)/shard_map/all_to_all | solution.py:467
  738.9 4.5 convert_bitcast_fusion
  747.1 7.9 copy.88
  755.0 5.6 copy.91
  760.7 6.0 fusion.8
  766.8 89.2 %all-gather.2 = f32[32,1,2176]{2,1,0:T(1,128)} all-gather(f32[1,1,2176]{2,1,0:T(1,128)S(1)} %reshape.144), channel_id=3, replica_groups=mesh['shard'=2,'context'=4,'tensor'=4] {'shard','context','tensor'}, dimensions={0}, use_global_device_ids=true | all-gather | bytes 287232 | tf_op jit(solution)/shard_map/all_gather | solution.py:492
  871.7 19.7 %reduce-scatter.14.cloned.1.call-done = bf16[1,128,768]{1,2,0:T(8,128)(2,1)} async-done(((bf16[4,128,768]{1,2,0:T(8,128)(2,1)}), bf16[1,128,768]{1,2,0:T(8,128)(2,1)}) %reduce-scatter.14.cloned.1.call-update) | async-done | bytes 196624 | tf_op jit(solution)/shard_map/reduce_scatter | solution.py:486
  (189 shorter events, 78.5 us)
Async XLA Ops:
  7.2 59.6 %copy-start.19 = (bf16[128,1152]{1,0:T(8,128)(2,1)S(1)}, bf16[128,1152]{1,0:T(8,128)(2,1)}, u32[]{:S(2)}) copy-start(bf16[128,1152]{1,0:T(8,128)(2,1)} %param.24) | copy-start | bytes 884740
  7.2 59.6 %copy-start.18 = (bf16[128,1152]{1,0:T(8,128)(2,1)S(1)}, bf16[128,1152]{1,0:T(8,128)(2,1)}, u32[]{:S(2)}) copy-start(bf16[128,1152]{1,0:T(8,128)(2,1)} %param.25) | copy-start | bytes 884740
  7.2 59.5 %all-gather.8.cloned.1.call-start = ((), (), s32[]{:S(2)}) async-start(), calls=%async_computation.9 | async-start | bytes 4718592 | tf_op jit(solution)/shard_map/all_gather | solution.py:373
  8.2 59.5 %copy-start.4 = (bf16[512,1024]{1,0:T(8,128)(2,1)S(1)}, bf16[512,1024]{1,0:T(8,128)(2,1)}, u32[]{:S(2)}) copy-start(bf16[512,1024]{1,0:T(8,128)(2,1)} %param.14) | copy-start | bytes 3145732
  29.7 39.5 %copy-start.26 = (f32[1024]{0:T(1024)S(1)}, f32[1024]{0:T(1024)}, u32[]{:S(2)}) copy-start(f32[1024]{0:T(1024)} %param.16) | copy-start | bytes 12292
  30.5 150.4 %all-gather.10.cloned.1.call-start = ((), (), s32[]{:S(2)}) async-start(), calls=%async_computation.10 | async-start | bytes 2359296 | tf_op jit(solution)/shard_map/all_gather | solution.py:384
  66.8 148.3 %all-gather.12.cloned.1.call-start = ((), (), s32[]{:S(2)}) async-start(), calls=%async_computation.11 | async-start | bytes 5308416 | tf_op jit(solution)/shard_map/all_gather | solution.py:385
  75.2 5.8 copy-start.28
  75.2 5.8 copy-start.29
  75.2 35.9 %all-to-all-start = ((bf16[4,512,512]{1,2,0:T(8,128)(2,1)}), bf16[4,512,512]{1,2,0:T(8,128)(2,1)}, u32[]{:S(2)}, u32[]{:S(2)}) async-start(bf16[4,512,512]{1,2,0:T(8,128)(2,1)} %convert_bitcast_fusion.2), calls=%async_computation | async-start | bytes 4194304 | tf_op jit(solution)/shard_map/all_to_all | solution.py:393
  79.8 157.0 %all-gather.14.cloned.1.call-start = ((), (), s32[]{:S(2)}) async-start(), calls=%async_computation.12 | async-start | bytes 2654208 | tf_op jit(solution)/shard_map/all_gather | solution.py:388
  86.7 629.8 %reduce-scatter.16.cloned.1.call-start = ((), (), s32[]{:S(2)}) async-start(), calls=%async_computation.15 | async-start | bytes 2654208
  187.0 27.3 %collective-permute-start.7 = (bf16[512,1024]{1,0:T(8,128)(2,1)}, bf16[512,1024]{1,0:T(8,128)(2,1)}, u32[]{:S(2)}, u32[]{:S(2)}) collective-permute-start(bf16[512,1024]{1,0:T(8,128)(2,1)} %multiply_convert_fusion.12), channel_id=1, source_target_pairs={{0,3},{1,0},{2,1},{3,2},{4,7},{5,4},{6,5},{7,6},{8,11},{9,8},{10,9... | collective-permute-start | bytes 3145736 | tf_op jit(solution)/shard_map/ppermute | solution.py:369
  190.3 46.5 %collective-permute-start.6 = (bf16[512,1024]{1,0:T(8,128)(2,1)}, bf16[512,1024]{1,0:T(8,128)(2,1)}, u32[]{:S(2)}, u32[]{:S(2)}) collective-permute-start(bf16[512,1024]{1,0:T(8,128)(2,1)} %param.27), channel_id=1, source_target_pairs={{0,3},{1,0},{2,1},{3,2},{4,7},{5,4},{6,5},{7,6},{8,11},{9,8},{10,9... | collective-permute-start | bytes 3145736 | tf_op jit(solution)/shard_map/ppermute | solution.py:369
  190.9 227.7 %collective-permute-start.3 = (bf16[512,1024]{1,0:T(8,128)(2,1)}, bf16[512,1024]{1,0:T(8,128)(2,1)}, u32[]{:S(2)}, u32[]{:S(2)}) collective-permute-start(bf16[512,1024]{1,0:T(8,128)(2,1)} %param.27), channel_id=1, source_target_pairs={{0,2},{1,3},{2,0},{3,1},{4,6},{5,7},{6,4},{7,5},{8,10},{9,11},{10,... | collective-permute-start | bytes 3145736 | tf_op jit(solution)/shard_map/ppermute | solution.py:369
  190.9 238.7 %collective-permute-start = (bf16[512,1024]{1,0:T(8,128)(2,1)}, bf16[512,1024]{1,0:T(8,128)(2,1)}, u32[]{:S(2)}, u32[]{:S(2)}) collective-permute-start(bf16[512,1024]{1,0:T(8,128)(2,1)} %param.27), channel_id=1, source_target_pairs={{0,1},{1,2},{2,3},{3,0},{4,5},{5,6},{6,7},{7,4},{8,9},{9,10},{10,1... | collective-permute-start | bytes 3145736 | tf_op jit(solution)/shard_map/ppermute | solution.py:369
  192.4 222.3 %collective-permute-start.4 = (bf16[512,1024]{1,0:T(8,128)(2,1)}, bf16[512,1024]{1,0:T(8,128)(2,1)}, u32[]{:S(2)}, u32[]{:S(2)}) collective-permute-start(bf16[512,1024]{1,0:T(8,128)(2,1)} %multiply_convert_fusion.12), channel_id=1, source_target_pairs={{0,2},{1,3},{2,0},{3,1},{4,6},{5,7},{6,4},{7,5},{8,10},{9,11},{10,... | collective-permute-start | bytes 3145736 | tf_op jit(solution)/shard_map/ppermute | solution.py:369
  214.3 211.3 %collective-permute-start.1 = (bf16[512,1024]{1,0:T(8,128)(2,1)}, bf16[512,1024]{1,0:T(8,128)(2,1)}, u32[]{:S(2)}, u32[]{:S(2)}) collective-permute-start(bf16[512,1024]{1,0:T(8,128)(2,1)} %multiply_convert_fusion.12), channel_id=1, source_target_pairs={{0,1},{1,2},{2,3},{3,0},{4,5},{5,6},{6,7},{7,4},{8,9},{9,10},{10,1... | collective-permute-start | bytes 3145736 | tf_op jit(solution)/shard_map/ppermute | solution.py:369
  236.8 5.7 copy-start.30
  242.5 206.5 %copy-start.7 = (bf16[512,1152]{1,0:T(8,128)(2,1)}, bf16[512,1152]{1,0:T(8,128)(2,1)S(1)}, u32[]{:S(2)}) copy-start(bf16[512,1152]{1,0:T(8,128)(2,1)S(1)} %get-tuple-element.103) | copy-start | bytes 3538948
  246.1 172.4 %copy-start.31 = (bf16[1024,1152]{1,0:T(8,128)(2,1)S(1)}, bf16[1024,1152]{1,0:T(8,128)(2,1)}, u32[]{:S(2)}) copy-start(bf16[1024,1152]{1,0:T(8,128)(2,1)} %all-gather.14.cloned.1.call-done) | copy-start | bytes 7077892
  246.1 224.1 %collective-permute-start.8 = (bf16[512,1024]{1,0:T(8,128)(2,1)}, bf16[512,1024]{1,0:T(8,128)(2,1)}, u32[]{:S(2)}, u32[]{:S(2)}) collective-permute-start(bf16[512,1024]{1,0:T(8,128)(2,1)} %fusion.23), channel_id=1, source_target_pairs={{0,1},{1,2},{2,3},{3,0},{4,5},{5,6},{6,7},{7,4},{8,9},{9,10},{10,1... | collective-permute-start | bytes 3145736 | tf_op jit(solution)/shard_map/ppermute | solution.py:369
  422.0 32.4 %copy-start.15 = (bf16[512,1152]{1,0:T(8,128)(2,1)}, bf16[512,1152]{1,0:T(8,128)(2,1)S(1)}, u32[]{:S(2)}) copy-start(bf16[512,1152]{1,0:T(8,128)(2,1)S(1)} %get-tuple-element.104) | copy-start | bytes 3538948
  425.7 44.5 %collective-permute-start.5 = (bf16[512,1024]{1,0:T(8,128)(2,1)}, bf16[512,1024]{1,0:T(8,128)(2,1)}, u32[]{:S(2)}, u32[]{:S(2)}) collective-permute-start(bf16[512,1024]{1,0:T(8,128)(2,1)} %fusion.22), channel_id=1, source_target_pairs={{0,2},{1,3},{2,0},{3,1},{4,6},{5,7},{6,4},{7,5},{8,10},{9,11},{10,... | collective-permute-start | bytes 3145736 | tf_op jit(solution)/shard_map/ppermute | solution.py:369
  433.0 18.6 %copy-start.6 = (bf16[512,1152]{1,0:T(8,128)(2,1)}, bf16[512,1152]{1,0:T(8,128)(2,1)S(1)}, u32[]{:S(2)}) copy-start(bf16[512,1152]{1,0:T(8,128)(2,1)S(1)} %get-tuple-element.105) | copy-start | bytes 3538948
  436.7 35.9 %collective-permute-start.2 = (bf16[512,1024]{1,0:T(8,128)(2,1)}, bf16[512,1024]{1,0:T(8,128)(2,1)}, u32[]{:S(2)}, u32[]{:S(2)}) collective-permute-start(bf16[512,1024]{1,0:T(8,128)(2,1)} %fusion.21), channel_id=1, source_target_pairs={{0,3},{1,0},{2,1},{3,2},{4,7},{5,4},{6,5},{7,6},{8,11},{9,8},{10,9... | collective-permute-start | bytes 3145736 | tf_op jit(solution)/shard_map/ppermute | solution.py:369
  463.0 280.4 %reduce-scatter.18.cloned.1.call-start = ((), (), s32[]{:S(2)}) async-start(), calls=%async_computation.16 | async-start | bytes 2359296
  467.0 5.6 slice-start
  472.7 9.0 copy-start.10
  477.7 28.0 %collective-permute-start.11 = (bf16[512,1024]{1,0:T(8,128)(2,1)S(1)}, bf16[512,1024]{1,0:T(8,128)(2,1)S(1)}, u32[]{:S(2)}, u32[]{:S(2)}) collective-permute-start(bf16[512,1024]{1,0:T(8,128)(2,1)S(1)} %convolution_convert_fusion.1), channel_id=1, source_target_pairs={{0,1},{1,2},{2,3},{3,0},{4,5},{5,6},{6,7},{7,4},{8,9},{9,10},{10,1... | collective-permute-start | bytes 3145736 | tf_op jit(solution)/shard_map/ppermute | solution.py:369
  478.3 71.4 %collective-permute-start.10 = (bf16[512,1024]{1,0:T(8,128)(2,1)S(1)}, bf16[512,1024]{1,0:T(8,128)(2,1)S(1)}, u32[]{:S(2)}, u32[]{:S(2)}) collective-permute-start(bf16[512,1024]{1,0:T(8,128)(2,1)S(1)} %convolution_convert_fusion.2), channel_id=1, source_target_pairs={{0,2},{1,3},{2,0},{3,1},{4,6},{5,7},{6,4},{7,5},{8,10},{9,11},{10,... | collective-permute-start | bytes 3145736 | tf_op jit(solution)/shard_map/ppermute | solution.py:369
  480.7 69.0 %collective-permute-start.9 = (bf16[512,1024]{1,0:T(8,128)(2,1)S(1)}, bf16[512,1024]{1,0:T(8,128)(2,1)S(1)}, u32[]{:S(2)}, u32[]{:S(2)}) collective-permute-start(bf16[512,1024]{1,0:T(8,128)(2,1)S(1)} %convolution_convert_fusion.3), channel_id=1, source_target_pairs={{0,3},{1,0},{2,1},{3,2},{4,7},{5,4},{6,5},{7,6},{8,11},{9,8},{10,9... | collective-permute-start | bytes 3145736 | tf_op jit(solution)/shard_map/ppermute | solution.py:369
  483.8 70.8 %copy-start.17 = (bf16[4,512,256]{2,1,0:T(8,128)(2,1)S(1)}, bf16[4,512,256]{2,1,0:T(8,128)(2,1)}, u32[]{:S(2)}) copy-start(bf16[4,512,256]{2,1,0:T(8,128)(2,1)} %all_to_all.20) | copy-start | bytes 3145732
  565.0 182.1 %reduce-scatter.12.cloned.1.call-start = ((), (), s32[]{:S(2)}) async-start(), calls=%async_computation.13 | async-start | bytes 5308416 | tf_op jit(solution)/shard_map/reduce_scatter | solution.py:432
  565.2 8.4 copy-start.34
  565.3 8.4 copy-start.36
  573.7 7.7 copy-start.38
  573.7 7.7 copy-start.40
  581.4 7.7 copy-start.12
  581.4 7.7 copy-start.14
  712.6 26.3 %copy-start.5 = (bf16[512,1024]{1,0:T(8,128)(2,1)S(1)}, bf16[512,1024]{1,0:T(8,128)(2,1)}, u32[]{:S(2)}) copy-start(bf16[512,1024]{1,0:T(8,128)(2,1)} %param.14) | copy-start | bytes 3145732
  712.6 26.3 %copy-start.25 = (f32[512]{0:T(512)S(1)}, f32[512]{0:T(512)}, u32[]{:S(2)}) copy-start(f32[512]{0:T(512)} %copy-done.24) | copy-start | bytes 6148
  712.6 26.3 %copy-start.27 = (f32[1024]{0:T(1024)S(1)}, f32[1024]{0:T(1024)}, u32[]{:S(2)}) copy-start(f32[1024]{0:T(1024)} %param.16) | copy-start | bytes 12292
  712.6 26.3 %all-to-all-start.3 = ((bf16[4,512,512]{2,1,0:T(8,128)(2,1)}), bf16[4,512,512]{2,1,0:T(8,128)(2,1)S(1)}, u32[]{:S(2)}, u32[]{:S(2)}) async-start(bf16[4,512,512]{2,1,0:T(8,128)(2,1)} %bitcast.18), calls=%async_computation.3 | async-start | bytes 4194304 | tf_op jit(solution)/shard_map/all_to_all | solution.py:467
  716.4 140.9 %reduce-scatter.20.cloned.1.call-start = ((), (), s32[]{:S(2)}) async-start(), calls=%async_computation.17 | async-start | bytes 4718592
  760.6 130.8 %reduce-scatter.14.cloned.1.call-start = ((), (), s32[]{:S(2)}) async-start(), calls=%async_computation.14 | async-start | bytes 983040 | tf_op jit(solution)/shard_map/reduce_scatter | solution.py:486
  856.0 8.4 copy-start.23
  856.0 9.1 %copy-start.3 = (f32[512,1024]{1,0:T(8,128)S(1)}, f32[512,1024]{1,0:T(8,128)}, u32[]{:S(2)}) copy-start(f32[512,1024]{1,0:T(8,128)} %copy-done.2) | copy-start | bytes 6291460
  (20 other events, 65.3 us)
Sparse Core Ops, SparseCore 0:
  30.6 36.0 all-gather.7
  69.2 38.6 all-gather.9
  110.3 43.6 all-gather.11
  155.7 34.1 all-gather.13
  463.1 43.5 reduce-scatter.15
  565.1 63.1 reduce-scatter.17
  631.7 51.7 reduce-scatter.11
  760.7 67.1 reduce-scatter.19
  864.0 27.3 reduce-scatter.13

commit v2 on v1

--- a/solution.py
+++ b/solution.py
@@ -38,7 +38,7 @@
     cosine, sine = jnp.cos(angles), jnp.sin(angles)
     wide = PAIR // (HEAD // 2)
     return (
-        starts[:, None],
+        starts.reshape(-1, BLK),
         jnp.concatenate([cosine] * wide, axis=1),
         jnp.concatenate([sine] * wide, axis=1),
     )
@@ -147,35 +147,55 @@
         lax.fori_loop(0, contexts * blocks, one, 0)
 
 
-def block_probs(dims, q_ref, cos_ref, sin_ref, start_ref, qgain_ref, keys):
-    window = dims[2]
+def for_reach(dims, body):
+    contexts, blocks, window = dims
+    block = pl.program_id(1)
+    total = contexts * blocks
+    widths = sorted({min(4 * BLK, window), min(8 * BLK, window), window})
+    lower = 0
+    for width in widths:
+        upper = total if width == window else width // BLK
+
+        @pl.when((block >= lower) & (block < upper))
+        def _(width=width):
+            body(width)
+
+        lower = upper
+
+
+def block_probs(width, q_ref, cos_ref, sin_ref, start_ref, qgain_ref, keys):
     block = pl.program_id(1)
     here = pl.ds(pl.multiple_of(block * BLK, BLK), BLK)
     query_raw = q_ref[...].astype(jnp.float32)
-    query = stacked(norm_rope(query_raw, qgain_ref[...], cos_ref[here, :], sin_ref[here, :]))
-    first = pl.multiple_of(jnp.maximum(block * BLK + BLK - window, 0), BLK)
-    span = pl.ds(first, window)
-    scores = product_cols(query, keys[span, :]) * (HEAD ** (-0.5))
-    shape = (BLK, window)
-    column = lax.broadcasted_iota(jnp.int32, shape, 1) + first
-    row = lax.broadcasted_iota(jnp.int32, shape, 0) + block * BLK
-    allowed = (column >= start_ref[here, :]) & (column <= row)
+    query_rot = norm_rope(query_raw, qgain_ref[...], cos_ref[here, :], sin_ref[here, :])
+    query = stacked(query_rot.astype(jnp.bfloat16).astype(jnp.float32) * (HEAD ** (-0.5)))
+    first = pl.multiple_of(jnp.maximum(block * BLK + BLK - width, 0), BLK)
+    span = pl.ds(first, width)
+    scores = product_cols(keys[span, :], query)
+    shape = (width, BLK)
+    key_place = lax.broadcasted_iota(jnp.int32, shape, 0) + first
+    query_place = lax.broadcasted_iota(jnp.int32, shape, 1) + block * BLK
+    allowed = (key_place >= start_ref[pl.ds(block, 1), :]) & (key_place <= query_place)
     offset = jnp.where(allowed, 0.0, -1e30)
-    scores = scores + jnp.concatenate([offset, offset], axis=0)
-    lifted = jnp.exp(scores - jnp.max(scores, axis=1, keepdims=True))
-    probs = lifted * (1.0 / jnp.sum(lifted, axis=1, keepdims=True))
-    return query_raw, query, span, here, probs
+    scores = scores + jnp.concatenate([offset, offset], axis=1)
+    lifted = jnp.exp(scores - jnp.max(scores, axis=0, keepdims=True))
+    total = jnp.sum(lifted, axis=0, keepdims=True)
+    return query_raw, query, span, here, lifted * (1.0 / total)
 
 
 def forward_kernel(
     dims, q_ref, k_ref, v_ref, cos_ref, sin_ref, start_ref, qgain_ref, kgain_ref, o_ref, keys, values
 ):
     prepare_keys(dims, k_ref, v_ref, cos_ref, sin_ref, kgain_ref, keys, values)
-    _, _, span, _, probs = block_probs(
-        dims, q_ref, cos_ref, sin_ref, start_ref, qgain_ref, keys
-    )
-    mixture = product(probs.astype(jnp.bfloat16), values[span, :])
-    o_ref[...] = unstacked(mixture).astype(o_ref.dtype)
+
+    def body(width):
+        _, _, span, _, probs = block_probs(
+            width, q_ref, cos_ref, sin_ref, start_ref, qgain_ref, keys
+        )
+        mixture = product_rows(values[span, :], probs.astype(jnp.bfloat16))
+        o_ref[...] = unstacked(mixture.T).astype(o_ref.dtype)
+
+    for_reach(dims, body)
 
 
 def backward_kernel(
@@ -215,21 +235,24 @@
         dqgain_ref[...] = jnp.zeros_like(dqgain_ref)
         dkgain_ref[...] = jnp.zeros_like(dkgain_ref)
 
-    query_raw, query, span, here, probs = block_probs(
-        dims, q_ref, cos_ref, sin_ref, start_ref, qgain_ref, keys
-    )
-    grad = stacked(d_ref[...].astype(jnp.float32))
-    d_probs = product_cols(grad, values[span, :])
-    row_dot = jnp.sum(probs * d_probs, axis=1, keepdims=True)
-    d_scores = (probs * (d_probs - row_dot)).astype(jnp.bfloat16)
-    value_acc[span, :] += product_rows(probs.astype(jnp.bfloat16), grad)
-    key_acc[span, :] += product_rows(d_scores, query)
-    d_query_rot = unstacked(product(d_scores, keys[span, :])) * scale
-    d_query, gain_grad = norm_rope_back(
-        d_query_rot, query_raw, qgain_ref[...], cos_ref[here, :], sin_ref[here, :]
-    )
-    dq_ref[...] = d_query.astype(dq_ref.dtype)
-    dqgain_ref[0:1, :] += gain_grad
+    def body(width):
+        query_raw, query, span, here, probs = block_probs(
+            width, q_ref, cos_ref, sin_ref, start_ref, qgain_ref, keys
+        )
+        grad = stacked(d_ref[...].astype(jnp.float32))
+        d_probs = product_cols(values[span, :], grad)
+        row_dot = jnp.sum(probs * d_probs, axis=0, keepdims=True)
+        d_scores = (probs * (d_probs - row_dot)).astype(jnp.bfloat16)
+        value_acc[span, :] += product(probs.astype(jnp.bfloat16), grad)
+        key_acc[span, :] += product(d_scores, query)
+        d_query_rot = unstacked(product_rows(keys[span, :], d_scores).T) * scale
+        d_query, gain_grad = norm_rope_back(
+            d_query_rot, query_raw, qgain_ref[...], cos_ref[here, :], sin_ref[here, :]
+        )
+        dq_ref[...] = d_query.astype(dq_ref.dtype)
+        dqgain_ref[0:1, :] += gain_grad
+
+    for_reach(dims, body)
 
     @pl.when(block == contexts * blocks - 1)
     def _():
@@ -240,7 +263,7 @@
             stream = pl.ds(pl.multiple_of(item * BLK, BLK), BLK)
             raw = twice(k_ref[place, :].astype(jnp.float32), which)
             d_key_rot = key_acc[stream, :]
-            d_key_rot = (d_key_rot + pltpu.roll(d_key_rot, HEAD, 1)) * scale
+            d_key_rot = d_key_rot + pltpu.roll(d_key_rot, HEAD, 1)
             d_key, key_gain_grad = norm_rope_back(
                 d_key_rot, raw, kgain_ref[...], cos_ref[stream, :], sin_ref[stream, :]
             )
@@ -281,7 +304,7 @@
         whole(tall, pairs + 1),
         whole(tall),
         whole(tall),
-        whole((rows, 1)),
+        whole((stream_blocks, BLK)),
         whole((1, PAIR)),
         whole((1, PAIR)),
     ]
@@ -395,6 +418,7 @@
     mixed = attention(
         False, contexts, qkv, cosine, sine, starts, query_gain, key_gain, None
     )
+    mixed, *grad_rows = lax.optimization_barrier((mixed, *grad_rows))
     attended = lax.all_to_all(
         mixed.reshape(contexts, tok_rows, query_cols),
         "context",
@@ -412,6 +436,10 @@
     outputs_part, grads_part = [], []
     pair_grad = down_grad = None
     for step in range(tensors):
+        if step > 0:
+            normed_rows[step], pair_grad, down_grad = lax.optimization_barrier(
+                (normed_rows[step], pair_grad, down_grad)
+            )
         pre = product(normed_rows[step], pair_weight)
         d_activated = product(grad_rows[step], down_full)
         gate_pre, up_pre = pre[:, :hidden], pre[:, hidden:]
@@ -439,10 +467,7 @@
     d_normed_mid, *late = lax.optimization_barrier(
         (d_normed_mid, *[part.astype(bfloat) for part in outputs_part[1:]])
     )
-    ffn_output = outputs_part[0]
-    for step in range(1, tensors):
-        ffn_output = ffn_output + shift(late[step - 1], -step).astype(jnp.float32)
-    block_output = hidden_in + ffn_output
+    returned = [shift(late[step - 1], -step) for step in range(1, tensors)]
 
     d_hidden_mid, feedforward_gain_grad = mid_pull(d_normed_mid)
     d_hidden = cotangent.astype(jnp.float32) + d_hidden_mid
@@ -461,6 +486,13 @@
     d_query_here, d_key_here, d_value_here, query_gain_rows, key_gain_rows = attention(
         True, contexts, qkv, cosine, sine, starts, query_gain, key_gain, d_attended
     )
+    d_query_here, d_key_here, d_value_here, *returned = lax.optimization_barrier(
+        (d_query_here, d_key_here, d_value_here, *returned)
+    )
+    ffn_output = outputs_part[0]
+    for part in returned:
+        ffn_output = ffn_output + part.astype(jnp.float32)
+    block_output = hidden_in + ffn_output
     query_gain_grad = query_gain_rows[0, :HEAD] + query_gain_rows[0, HEAD:]
     key_gain_grad = key_gain_rows[0, :HEAD]
     d_qkv_send = jnp.concatenate([d_query_here, d_key_here, d_value_here], axis=1)
@@ -489,8 +521,14 @@
     gains = jnp.concatenate(
         [attention_gain_grad, feedforward_gain_grad, query_gain_grad, key_gain_grad]
     )
-    gains = lax.all_gather(gains[None, :], ("shard", "context", "tensor"), axis=0, tiled=True)
-    gains = jnp.sum(gains, axis=0)
+    gains = gains.reshape(-1, PAIR)
+    for axis in ("shard", "context", "tensor"):
+        size = lax.axis_size(axis)
+        reach = 1
+        while reach < size:
+            gains = gains + lax.ppermute(gains, axis, [(i, i ^ reach) for i in range(size)])
+            reach *= 2
+    gains = gains.reshape(-1)
     pair_owned = pair_owned.astype(jnp.float32)
     return (
         block_output,

time: 911 us -> 733 us (0.80)
  blocking collectives: 151 us -> 78.9 us
  waiting for transfers between devices: 253 us -> 188 us
  starting transfers between devices: 135 us -> 75.9 us
  other arithmetic: 28.6 us -> 66.8 us
  local copies, waits for them, and re-layouts: 54.7 us -> 45 us
    all_gather x1 -> x0, blocking collectives: 89.2 us -> none  [on_device(): lax.all_gather(gains[None, :], ('shard', 'context', 'tensor'), axis=0, ti...]
    ppermute x12, waiting for transfers between devices: 157 us -> 76.2 us  [shift(): return lax.ppermute(values, 'tensor', pairs)]
    ppermute x12, starting transfers between devices: 126 us -> 60.1 us  [shift(): return lax.ppermute(values, 'tensor', pairs)]
    unnamed x12 -> x11, waiting for transfers between devices: 0.19 us -> 32 us
    add x0 -> x10, other arithmetic: none -> 31.7 us  [the longest x2 22.4 us: on_device(): pair_grad = pair_term if step == 0 else pair_grad + pair_term]
    convert_element_type x0 -> x3, other arithmetic: none -> 15.2 us  [the longest x1 9.69 us: on_device(): pair_grad.astype(bfloat)]
    all_to_all x1, blocking collectives: 20.8 us -> 34.8 us  [on_device(): lax.all_to_all(d_qkv_send.reshape(contexts, tok_rows, qkv_cols), 'context...]
    all_to_all x1, waiting for transfers between devices: 21.3 us -> 10.2 us  [on_device(): lax.all_to_all(d_attended_send, 'context', split_axis=0, concat_axis=0, t...]
  transfers between devices with their start and end apart: 23 -> 28, of which waited for: 10 -> 10; matrix products, arithmetic and copies ran while one was open for 21% -> 28% of each run, Pallas kernels for 14% -> 17%
where the time goes in v2:
time: 733 us; the launch traced here: 727 us
  waiting for transfers between devices  188 us (26%)
  matrix products  134 us (18%)
  Pallas kernels  123 us (17%)
  blocking collectives  78.9 us (11%)
  starting transfers between devices  75.9 us (10%)
  other arithmetic  66.8 us (9%)
  local copies, waits for them, and re-layouts  45 us (6%)
  between operations  14.8 us (2%)
    pallas_call x1, Pallas kernels, attention(): pl.pallas_call(lambda *refs: backward_kernel(dims, *refs), grid=(pairs, s...  76.3 us
    ppermute x12, waiting for transfers between devices, shift(): return lax.ppermute(values, 'tensor', pairs)  76.2 us
    ppermute x12, starting transfers between devices, shift(): return lax.ppermute(values, 'tensor', pairs)  60.1 us
    pallas_call x1, Pallas kernels, attention(): pl.pallas_call(lambda *refs: forward_kernel(dims, *refs), grid=(pairs, st...  46.9 us
    dot_general x8, matrix products, product_rows(): lax.dot_general(left, right, contract_rows, preferred_element_type=jnp.fl...  43.2 us
    dot_general x8, matrix products, product(): return jnp.dot(left, right, preferred_element_type=jnp.float32)  38.1 us
    unnamed x113, local copies, waits for them, and re-layouts  36.4 us
    all_gather x1, waiting for transfers between devices, on_device(): lax.all_gather(attn_cols[:, :, :qkv_cols], rows_axes, axis=1, tiled=True)  35.5 us
  transfers between devices with their start and end apart: 28, of which 10 were waited for; matrix products, arithmetic and copies ran while one was open for 28% of the time, Pallas kernels for 17%

profile of v2, /device:TPU:0, one launch (start us, length us, event | category | flops | bytes accessed | tf_op | source)
XLA Modules:
  0.0 727.2 jit_solution(8436056392509913617)
XLA Ops:
  8.2 21.4 %all-gather = bf16[512,768]{1,0:T(8,128)(2,1)S(1)} all-gather(bf16[128,768]{1,0:T(8,128)(2,1)S(1)} %pad_maximum_fusion.25), channel_id=2, replica_groups=mesh['shard'=2,'context'=4,'tensor'=4] {'tensor'}, dimensions={0}, use_global_device_ids=true | all-gather | bytes 983040 | tf_op jit(solution)/shard_map/all_gather | solution.py:395
  31.3 35.5 %all-gather.6.cloned.1.call-done = bf16[4,1024,512]{2,1,0:T(8,128)(2,1)} async-done(((bf16[4,128,512]{2,1,0:T(8,128)(2,1)}), bf16[4,1024,512]{2,1,0:T(8,128)(2,1)}) %all-gather.6.cloned.1.call-update) | async-done | bytes 4194320 | tf_op jit(solution)/shard_map/all_gather | solution.py:396
  69.2 6.0 convert_bitcast_fusion.2
  75.2 4.6 all-to-all-start
  79.8 3.4 collective-permute-start.2
  85.8 3.7 multiply_sine_fusion
  92.2 18.8 %all-to-all-done = bf16[4,512,512]{1,2,0:T(8,128)(2,1)} async-done(((bf16[4,512,512]{1,2,0:T(8,128)(2,1)}), bf16[4,512,512]{1,2,0:T(8,128)(2,1)}, u32[]{:S(2)}, u32[]{:S(2)}) %all-to-all-start) | async-done | bytes 2097184 | tf_op jit(solution)/shard_map/all_to_all | solution.py:416
  115.8 46.9 %attention_forward.1 = bf16[2048,256]{1,0:T(8,128)(2,1)S(1)} custom-call(bf16[2048,512]{1,0:T(8,128)(2,1)S(1)} %bitcast.117, bf16[2048,512]{1,0:T(8,128)(2,1)S(1)} %bitcast.118, bf16[2048,512]{1,0:T(8,128)(2,1)S(1)} %bitcast.119, f32[2048,128]{1,0:T(8,128)S(1)} %get-tuple-element.161.refs_3_, f32[2048,128]{1,0:T(8,128)S(1)} %copy-done.1, ...), custom_call_target="tpu_custom_call" | custom-call | flops 4831838208 | bytes 10485760 | tf_op jit(solution)/shard_map/attention_forward/pallas_call | solution.py:327
  162.8 11.1 %collective-permute-done.1 = bf16[512,1024]{1,0:T(8,128)(2,1)} collective-permute-done((bf16[512,1024]{1,0:T(8,128)(2,1)}, bf16[512,1024]{1,0:T(8,128)(2,1)}, u32[]{:S(2)}, u32[]{:S(2)}) %collective-permute-start.1) | collective-permute-done | bytes 1048608 | tf_op jit(solution)/shard_map/ppermute | solution.py:392
  173.9 22.7 %all_to_all.20 = bf16[4,512,256]{2,1,0:T(8,128)(2,1)} all-to-all(bf16[4,512,256]{2,1,0:T(8,128)(2,1)S(1)} %bitcast.124), channel_id=1, replica_groups=mesh['shard'=2,'context'=4,'tensor'=4] {'context'}, dimensions={0} | all-to-all | bytes 2097152 | tf_op jit(solution)/shard_map/all_to_all | solution.py:422
  196.5 3.6 multiply_reduce_fusion.2
  206.2 7.4 %fusion.46 = f32[512,2304]{1,0:T(8,128)} fusion(bf16[512,1024]{1,0:T(8,128)(2,1)} %multiply_convert_fusion.12, bf16[1024,2304]{1,0:T(8,128)(2,1)} %all-gather.10.cloned.1.call-done), kind=kOutput, calls=%fused_computation.114 | convolution fusion | flops 2415919104 | bytes 10485760 | tf_op jit(solution)/shard_map/dot_general | solution.py:48
  213.6 5.5 multiply_convert_fusion.10
  219.1 3.8 fusion.48
  222.9 7.6 %fusion.18 = f32[1024,2304]{1,0:T(8,128)} fusion(bf16[512,1024]{1,0:T(8,128)(2,1)} %multiply_convert_fusion.12, bf16[512,1152]{1,0:T(8,128)(2,1)S(1)} %get-tuple-element.141, bf16[512,1152]{1,0:T(8,128)(2,1)S(1)} %get-tuple-element.140), kind=kOutput, calls=%fused_computation.58 | convolution fusion | flops 2420637696 | bytes 12845056 | tf_op jit(solution)/shard_map/dot_general | solution.py:56
  230.5 42.4 %collective-permute-done.3 = bf16[512,1024]{1,0:T(8,128)(2,1)} collective-permute-done((bf16[512,1024]{1,0:T(8,128)(2,1)}, bf16[512,1024]{1,0:T(8,128)(2,1)}, u32[]{:S(2)}, u32[]{:S(2)}) %collective-permute-start.3) | collective-permute-done | bytes 1048608 | tf_op jit(solution)/shard_map/ppermute | solution.py:392
  272.9 3.8 fusion.49
  276.8 3.4 multiply_convert_fusion.8
  280.2 4.0 fusion.20
  289.6 7.5 %fusion.16 = f32[1024,2304]{1,0:T(8,128)} fusion(bf16[512,1024]{1,0:T(8,128)(2,1)} %collective-permute-done.3, bf16[512,1152]{1,0:T(8,128)(2,1)S(1)} %get-tuple-element.139, bf16[512,1152]{1,0:T(8,128)(2,1)S(1)} %get-tuple-element.138), kind=kOutput, calls=%fused_computation.56 | convolution fusion | flops 2420637696 | bytes 12845056 | tf_op jit(solution)/shard_map/dot_general | solution.py:56
  297.1 11.2 %add.132 = f32[1024,2304]{1,0:T(8,128)} add(f32[1024,2304]{1,0:T(8,128)} %fusion.18, f32[1024,2304]{1,0:T(8,128)} %fusion.16) | non-fusion elementwise | flops 2359296 | bytes 28311552 | tf_op jit(solution)/shard_map/add | solution.py:458
  308.3 5.4 fusion.51
  313.7 3.6 multiply_convert_fusion.5
  317.4 3.6 fusion.21
  321.0 44.1 %collective-permute-start.6 = (bf16[512,1024]{1,0:T(8,128)(2,1)}, bf16[512,1024]{1,0:T(8,128)(2,1)}, u32[]{:S(2)}, u32[]{:S(2)}) collective-permute-start(bf16[512,1024]{1,0:T(8,128)(2,1)} %fusion.21), channel_id=1, source_target_pairs={{0,2},{1,3},{2,0},{3,1},{4,6},{5,7},{6,4},{7,5},{8,10},{9,11},{10,... | collective-permute-start | bytes 3145736 | tf_op jit(solution)/shard_map/ppermute | solution.py:392
  370.8 7.5 %fusion.14 = f32[1024,2304]{1,0:T(8,128)} fusion(bf16[512,1024]{1,0:T(8,128)(2,1)} %collective-permute-done.5, bf16[512,1152]{1,0:T(8,128)(2,1)S(1)} %get-tuple-element.137, bf16[512,1152]{1,0:T(8,128)(2,1)S(1)} %get-tuple-element.136), kind=kOutput, calls=%fused_computation.54 | convolution fusion | flops 2420637696 | bytes 12845056 | tf_op jit(solution)/shard_map/dot_general | solution.py:56
  378.3 11.2 %add.137 = f32[1024,2304]{1,0:T(8,128)} add(f32[1024,2304]{1,0:T(8,128)} %add.132, f32[1024,2304]{1,0:T(8,128)} %fusion.14) | non-fusion elementwise | flops 2359296 | bytes 28311552 | tf_op jit(solution)/shard_map/add | solution.py:458
  389.5 5.4 fusion.53
  394.9 3.5 multiply_convert_fusion.2
  412.0 21.7 %collective-permute-done.6 = bf16[512,1024]{1,0:T(8,128)(2,1)} collective-permute-done((bf16[512,1024]{1,0:T(8,128)(2,1)}, bf16[512,1024]{1,0:T(8,128)(2,1)}, u32[]{:S(2)}, u32[]{:S(2)}) %collective-permute-start.6) | collective-permute-done | bytes 1048608 | tf_op jit(solution)/shard_map/ppermute | solution.py:392
  433.7 4.4 convert_add_fusion.1
  452.9 4.6 add_convert_fusion.1
  458.8 7.9 %fusion.12 = f32[1024,2304]{1,0:T(8,128)} fusion(bf16[512,1024]{1,0:T(8,128)(2,1)} %collective-permute-done.7, bf16[512,1152]{1,0:T(8,128)(2,1)} %copy-done.42, bf16[512,1152]{1,0:T(8,128)(2,1)S(1)} %copy-done.41), kind=kOutput, calls=%fused_computation.52 | convolution fusion | flops 2420637696 | bytes 12845056 | tf_op jit(solution)/shard_map/dot_general | solution.py:56
  466.7 9.7 %add_convert_fusion = bf16[1024,2304]{1,0:T(8,128)(2,1)} fusion(f32[1024,2304]{1,0:T(8,128)} %add.137, f32[1024,2304]{1,0:T(8,128)} %fusion.12), kind=kLoop, calls=%fused_computation | loop fusion | flops 4718592 | bytes 23592960 | tf_op jit(solution)/shard_map/convert_element_type | solution.py:461
  478.1 3.9 fusion.23
  482.0 4.4 all-to-all-start.2
  490.9 10.2 %all-to-all-done.2 = bf16[4,512,256]{1,2,0:T(8,128)(2,1)} async-done(((bf16[4,512,256]{1,2,0:T(8,128)(2,1)}), bf16[4,512,256]{1,2,0:T(8,128)(2,1)}, u32[]{:S(2)}, u32[]{:S(2)}) %all-to-all-start.2) | async-done | bytes 1048608 | tf_op jit(solution)/shard_map/all_to_all | solution.py:478
  502.7 76.3 %attention_backward.1 = (bf16[2048,256]{1,0:T(8,128)(2,1)S(1)}, bf16[2048,128]{1,0:T(8,128)(2,1)S(1)}, bf16[2048,128]{1,0:T(8,128)(2,1)S(1)}, f32[8,128]{1,0:T(8,128)S(1)}, f32[8,128]{1,0:T(8,128)S(1)}) custom-call(bf16[2048,512]{1,0:T(8,128)(2,1)} %bitcast.120, bf16[2048,512]{1,0:T(8,128)(2,1)} %bitcast.121, bf16[2048,512]{1,0:T(8,128)(2,1)} %bitcast.122, ...), custom_call_target="tpu_custom_call" | custom-call | flops 12079595520 | bytes 16777216 | tf_op jit(solution)/shard_map/attention_backward/pallas_call | solution.py:341
  580.2 34.8 %all_to_all.21 = bf16[4,512,512]{2,1,0:T(8,128)(2,1)S(1)} all-to-all(bf16[4,512,512]{2,1,0:T(8,128)(2,1)S(1)} %bitcast.130), channel_id=1, replica_groups=mesh['shard'=2,'context'=4,'tensor'=4] {'context'}, dimensions={0} | all-to-all | bytes 4194304 | tf_op jit(solution)/shard_map/all_to_all | solution.py:499
  616.3 4.5 convert_bitcast_fusion
  622.2 7.9 %copy.63 = bf16[4,1024,512]{2,0,1:T(4,128)(2,1)} copy(bf16[4,1024,512]{1,2,0:T(8,128)(2,1)} %convert_bitcast_fusion) | data formatting | bytes 8388608
  630.1 5.6 copy.66
  635.9 6.8 fusion.7
  644.8 3.5 fusion.47
  649.2 4.1 add_add_fusion.2
  654.8 31.9 %reduce-scatter.18.cloned.1.call-done = bf16[128,2048]{1,0:T(8,128)(2,1)} async-done(((bf16[1024,2048]{1,0:T(8,128)(2,1)}), bf16[128,2048]{1,0:T(8,128)(2,1)}) %reduce-scatter.18.cloned.1.call-update) | async-done | bytes 524304
  695.6 3.5 fusion.9
  702.3 14.2 %reduce-scatter.14.cloned.1.call-done = bf16[1,128,768]{1,2,0:T(8,128)(2,1)} async-done(((bf16[4,128,768]{1,2,0:T(8,128)(2,1)}), bf16[1,128,768]{1,2,0:T(8,128)(2,1)}) %reduce-scatter.14.cloned.1.call-update) | async-done | bytes 196624 | tf_op jit(solution)/shard_map/reduce_scatter | solution.py:518
  (220 shorter events, 94.0 us)
Async XLA Ops:
  7.2 59.6 %copy-start.21 = (bf16[128,1152]{1,0:T(8,128)(2,1)S(1)}, bf16[128,1152]{1,0:T(8,128)(2,1)}, u32[]{:S(2)}) copy-start(bf16[128,1152]{1,0:T(8,128)(2,1)} %param.25) | copy-start | bytes 884740
  7.2 59.6 %copy-start.22 = (bf16[128,1152]{1,0:T(8,128)(2,1)S(1)}, bf16[128,1152]{1,0:T(8,128)(2,1)}, u32[]{:S(2)}) copy-start(bf16[128,1152]{1,0:T(8,128)(2,1)} %param.24) | copy-start | bytes 884740
  7.2 59.5 %all-gather.6.cloned.1.call-start = ((), (), s32[]{:S(2)}) async-start(), calls=%async_computation.9 | async-start | bytes 4718592 | tf_op jit(solution)/shard_map/all_gather | solution.py:396
  8.2 59.5 %copy-start.8 = (bf16[512,1024]{1,0:T(8,128)(2,1)S(1)}, bf16[512,1024]{1,0:T(8,128)(2,1)}, u32[]{:S(2)}) copy-start(bf16[512,1024]{1,0:T(8,128)(2,1)} %param.14) | copy-start | bytes 3145732
  29.7 39.5 %copy-start.29 = (f32[1024]{0:T(1024)S(1)}, f32[1024]{0:T(1024)}, u32[]{:S(2)}) copy-start(f32[1024]{0:T(1024)} %param.16) | copy-start | bytes 12292
  30.5 166.0 %all-gather.8.cloned.1.call-start = ((), (), s32[]{:S(2)}) async-start(), calls=%async_computation.10 | async-start | bytes 2359296 | tf_op jit(solution)/shard_map/all_gather | solution.py:407
  66.8 139.4 %all-gather.10.cloned.1.call-start = ((), (), s32[]{:S(2)}) async-start(), calls=%async_computation.11 | async-start | bytes 5308416 | tf_op jit(solution)/shard_map/all_gather | solution.py:408
  75.2 35.8 %all-to-all-start = ((bf16[4,512,512]{1,2,0:T(8,128)(2,1)}), bf16[4,512,512]{1,2,0:T(8,128)(2,1)}, u32[]{:S(2)}, u32[]{:S(2)}) async-start(bf16[4,512,512]{1,2,0:T(8,128)(2,1)} %convert_bitcast_fusion.2), calls=%async_computation | async-start | bytes 4194304 | tf_op jit(solution)/shard_map/all_to_all | solution.py:416
  79.8 133.8 %all-gather.12.cloned.1.call-start = ((), (), s32[]{:S(2)}) async-start(), calls=%async_computation.12 | async-start | bytes 2654208 | tf_op jit(solution)/shard_map/all_gather | solution.py:411
  79.8 82.9 %collective-permute-start.2 = (bf16[512,1024]{1,0:T(8,128)(2,1)}, bf16[512,1024]{1,0:T(8,128)(2,1)}, u32[]{:S(2)}, u32[]{:S(2)}) collective-permute-start(bf16[512,1024]{1,0:T(8,128)(2,1)} %param.27), channel_id=1, source_target_pairs={{0,3},{1,0},{2,1},{3,2},{4,7},{5,4},{6,5},{7,6},{8,11},{9,8},{10,9... | collective-permute-start | bytes 3145736 | tf_op jit(solution)/shard_map/ppermute | solution.py:392
  83.3 90.6 %collective-permute-start.1 = (bf16[512,1024]{1,0:T(8,128)(2,1)}, bf16[512,1024]{1,0:T(8,128)(2,1)}, u32[]{:S(2)}, u32[]{:S(2)}) collective-permute-start(bf16[512,1024]{1,0:T(8,128)(2,1)} %param.27), channel_id=1, source_target_pairs={{0,2},{1,3},{2,0},{3,1},{4,6},{5,7},{6,4},{7,5},{8,10},{9,11},{10,... | collective-permute-start | bytes 3145736 | tf_op jit(solution)/shard_map/ppermute | solution.py:392
  83.3 90.6 %collective-permute-start = (bf16[512,1024]{1,0:T(8,128)(2,1)}, bf16[512,1024]{1,0:T(8,128)(2,1)}, u32[]{:S(2)}, u32[]{:S(2)}) collective-permute-start(bf16[512,1024]{1,0:T(8,128)(2,1)} %param.27), channel_id=1, source_target_pairs={{0,1},{1,2},{2,3},{3,0},{4,5},{5,6},{6,7},{7,4},{8,9},{9,10},{10,1... | collective-permute-start | bytes 3145736 | tf_op jit(solution)/shard_map/ppermute | solution.py:392
  85.0 535.8 %reduce-scatter.16.cloned.1.call-start = ((), (), s32[]{:S(2)}) async-start(), calls=%async_computation.16 | async-start | bytes 2359296
  113.8 48.9 %copy-start = (bf16[4,512,512]{2,1,0:T(8,128)(2,1)}, bf16[4,512,512]{2,1,0:T(8,128)(2,1)S(1)}, u32[]{:S(2)}) copy-start(bf16[4,512,512]{2,1,0:T(8,128)(2,1)S(1)} %copy.48) | copy-start | bytes 6291460
  200.1 238.7 %copy-start.3 = (f32[512,1024]{1,0:T(8,128)}, f32[512,1024]{1,0:T(8,128)S(1)}, u32[]{:S(2)}) copy-start(f32[512,1024]{1,0:T(8,128)S(1)} %get-tuple-element.159) | copy-start | bytes 6291460
  201.6 187.9 %collective-permute-start.7 = (bf16[512,1024]{1,0:T(8,128)(2,1)}, bf16[512,1024]{1,0:T(8,128)(2,1)}, u32[]{:S(2)}, u32[]{:S(2)}) collective-permute-start(bf16[512,1024]{1,0:T(8,128)(2,1)} %multiply_convert_fusion.12), channel_id=1, source_target_pairs={{0,3},{1,0},{2,1},{3,2},{4,7},{5,4},{6,5},{7,6},{8,11},{9,8},{10,9... | collective-permute-start | bytes 3145736 | tf_op jit(solution)/shard_map/ppermute | solution.py:392
  201.6 106.7 %collective-permute-start.5 = (bf16[512,1024]{1,0:T(8,128)(2,1)}, bf16[512,1024]{1,0:T(8,128)(2,1)}, u32[]{:S(2)}, u32[]{:S(2)}) collective-permute-start(bf16[512,1024]{1,0:T(8,128)(2,1)} %multiply_convert_fusion.12), channel_id=1, source_target_pairs={{0,2},{1,3},{2,0},{3,1},{4,6},{5,7},{6,4},{7,5},{8,10},{9,11},{10,... | collective-permute-start | bytes 3145736 | tf_op jit(solution)/shard_map/ppermute | solution.py:392
  204.5 68.4 %collective-permute-start.3 = (bf16[512,1024]{1,0:T(8,128)(2,1)}, bf16[512,1024]{1,0:T(8,128)(2,1)}, u32[]{:S(2)}, u32[]{:S(2)}) collective-permute-start(bf16[512,1024]{1,0:T(8,128)(2,1)} %multiply_convert_fusion.12), channel_id=1, source_target_pairs={{0,1},{1,2},{2,3},{3,0},{4,5},{5,6},{6,7},{7,4},{8,9},{9,10},{10,1... | collective-permute-start | bytes 3145736 | tf_op jit(solution)/shard_map/ppermute | solution.py:392
  219.1 53.8 %slice-start.2 = ((s8[4718592]{0:T(1024)(128)(4,1)}), s8[4194304]{0:T(1024)(128)(4,1)S(1)}, s32[]{:S(2)}) async-start(s8[4718592]{0:T(1024)(128)(4,1)} %bitcast.138), calls=%async_computation.20 | async-start | bytes 8388608
  222.9 50.0 %slice-start.3 = ((s8[4718592]{0:T(1024)(128)(4,1)}), s8[524288]{0:T(1024)(128)(4,1)S(1)}, s32[]{:S(2)}) async-start(s8[4718592]{0:T(1024)(128)(4,1)} %bitcast.138), calls=%async_computation.21 | async-start | bytes 1048576
  230.5 46.2 %copy-start.33 = (bf16[1024,1152]{1,0:T(8,128)(2,1)S(1)}, bf16[1024,1152]{1,0:T(8,128)(2,1)}, u32[]{:S(2)}) copy-start(bf16[1024,1152]{1,0:T(8,128)(2,1)} %all-gather.12.cloned.1.call-done) | copy-start | bytes 7077892
  284.2 127.8 %collective-permute-start.4 = (bf16[512,1024]{1,0:T(8,128)(2,1)}, bf16[512,1024]{1,0:T(8,128)(2,1)}, u32[]{:S(2)}, u32[]{:S(2)}) collective-permute-start(bf16[512,1024]{1,0:T(8,128)(2,1)} %fusion.20), channel_id=1, source_target_pairs={{0,3},{1,0},{2,1},{3,2},{4,7},{5,4},{6,5},{7,6},{8,11},{9,8},{10,9... | collective-permute-start | bytes 3145736 | tf_op jit(solution)/shard_map/ppermute | solution.py:392
  313.7 54.4 %slice-start = ((s8[4718592]{0:T(1024)(128)(4,1)}), s8[4194304]{0:T(1024)(128)(4,1)S(1)}, s32[]{:S(2)}) async-start(s8[4718592]{0:T(1024)(128)(4,1)} %bitcast.125), calls=%async_computation.18 | async-start | bytes 8388608
  317.3 47.8 %copy-start.17 = (bf16[512,1152]{1,0:T(8,128)(2,1)}, bf16[512,1152]{1,0:T(8,128)(2,1)S(1)}, u32[]{:S(2)}) copy-start(bf16[512,1152]{1,0:T(8,128)(2,1)S(1)} %get-tuple-element.143) | copy-start | bytes 3538948
  317.4 50.8 %slice-start.1 = ((s8[4718592]{0:T(1024)(128)(4,1)}), s8[524288]{0:T(1024)(128)(4,1)S(1)}, s32[]{:S(2)}) async-start(s8[4718592]{0:T(1024)(128)(4,1)} %bitcast.125), calls=%async_computation.19 | async-start | bytes 1048576
  321.0 112.7 %collective-permute-start.6 = (bf16[512,1024]{1,0:T(8,128)(2,1)}, bf16[512,1024]{1,0:T(8,128)(2,1)}, u32[]{:S(2)}, u32[]{:S(2)}) collective-permute-start(bf16[512,1024]{1,0:T(8,128)(2,1)} %fusion.21), channel_id=1, source_target_pairs={{0,2},{1,3},{2,0},{3,1},{4,6},{5,7},{6,4},{7,5},{8,10},{9,11},{10,... | collective-permute-start | bytes 3145736 | tf_op jit(solution)/shard_map/ppermute | solution.py:392
  402.1 31.6 %collective-permute-start.8 = (bf16[512,1024]{1,0:T(8,128)(2,1)S(1)}, bf16[512,1024]{1,0:T(8,128)(2,1)S(1)}, u32[]{:S(2)}, u32[]{:S(2)}) collective-permute-start(bf16[512,1024]{1,0:T(8,128)(2,1)S(1)} %fusion.22), channel_id=1, source_target_pairs={{0,1},{1,2},{2,3},{3,0},{4,5},{5,6},{6,7},{7,4},{8,9},{9,10},{10,1... | collective-permute-start | bytes 3145736 | tf_op jit(solution)/shard_map/ppermute | solution.py:392
  409.5 24.3 %copy-start.37 = (bf16[512,1152]{1,0:T(8,128)(2,1)S(1)}, bf16[512,1152]{1,0:T(8,128)(2,1)}, u32[]{:S(2)}) copy-start(bf16[512,1152]{1,0:T(8,128)(2,1)} %copy-done.36) | copy-start | bytes 3538948
  409.5 24.3 %copy-start.39 = (bf16[512,1152]{1,0:T(8,128)(2,1)S(1)}, bf16[512,1152]{1,0:T(8,128)(2,1)}, u32[]{:S(2)}) copy-start(bf16[512,1152]{1,0:T(8,128)(2,1)} %copy-done.38) | copy-start | bytes 3538948
  449.6 172.5 %reduce-scatter.12.cloned.1.call-start = ((), (), s32[]{:S(2)}) async-start(), calls=%async_computation.14 | async-start | bytes 2654208 | tf_op jit(solution)/shard_map/reduce_scatter | solution.py:463
  457.5 164.7 %reduce-scatter.10.cloned.1.call-start = ((), (), s32[]{:S(2)}) async-start(), calls=%async_computation.13 | async-start | bytes 5308416 | tf_op jit(solution)/shard_map/reduce_scatter | solution.py:460
  482.0 20.7 %copy-start.2 = (f32[2048,128]{1,0:T(8,128)S(1)}, f32[2048,128]{1,0:T(8,128)}, u32[]{:S(2)}) copy-start(f32[2048,128]{1,0:T(8,128)} %get-tuple-element.162.refs_4_) | copy-start | bytes 3145732
  482.0 19.2 %all-to-all-start.2 = ((bf16[4,512,256]{1,2,0:T(8,128)(2,1)}), bf16[4,512,256]{1,2,0:T(8,128)(2,1)}, u32[]{:S(2)}, u32[]{:S(2)}) async-start(bf16[4,512,256]{1,2,0:T(8,128)(2,1)} %fusion.23), calls=%async_computation.2 | async-start | bytes 2097152 | tf_op jit(solution)/shard_map/all_to_all | solution.py:478
  486.4 200.3 %reduce-scatter.18.cloned.1.call-start = ((), (), s32[]{:S(2)}) async-start(), calls=%async_computation.17 | async-start | bytes 4718592
  486.4 92.5 %collective-permute-start.9 = (bf16[512,1024]{1,0:T(8,128)(2,1)}, bf16[512,1024]{1,0:T(8,128)(2,1)}, u32[]{:S(2)}, u32[]{:S(2)}) collective-permute-start(bf16[512,1024]{1,0:T(8,128)(2,1)} %convolution_convert_fusion.3), channel_id=1, source_target_pairs={{0,3},{1,0},{2,1},{3,2},{4,7},{5,4},{6,5},{7,6},{8,11},{9,8},{10,9... | collective-permute-start | bytes 3145736 | tf_op jit(solution)/shard_map/ppermute | solution.py:392
  489.8 90.1 %collective-permute-start.10 = (bf16[512,1024]{1,0:T(8,128)(2,1)}, bf16[512,1024]{1,0:T(8,128)(2,1)}, u32[]{:S(2)}, u32[]{:S(2)}) collective-permute-start(bf16[512,1024]{1,0:T(8,128)(2,1)} %convolution_convert_fusion.2), channel_id=1, source_target_pairs={{0,2},{1,3},{2,0},{3,1},{4,6},{5,7},{6,4},{7,5},{8,10},{9,11},{10,... | collective-permute-start | bytes 3145736 | tf_op jit(solution)/shard_map/ppermute | solution.py:392
  489.8 90.1 %collective-permute-start.11 = (bf16[512,1024]{1,0:T(8,128)(2,1)}, bf16[512,1024]{1,0:T(8,128)(2,1)}, u32[]{:S(2)}, u32[]{:S(2)}) collective-permute-start(bf16[512,1024]{1,0:T(8,128)(2,1)} %convolution_convert_fusion.1), channel_id=1, source_target_pairs={{0,1},{1,2},{2,3},{3,0},{4,5},{5,6},{6,7},{7,4},{8,9},{9,10},{10,1... | collective-permute-start | bytes 3145736 | tf_op jit(solution)/shard_map/ppermute | solution.py:392
  580.1 36.2 %copy-start.9 = (bf16[512,1024]{1,0:T(8,128)(2,1)S(1)}, bf16[512,1024]{1,0:T(8,128)(2,1)}, u32[]{:S(2)}) copy-start(bf16[512,1024]{1,0:T(8,128)(2,1)} %param.14) | copy-start | bytes 3145732
  580.1 36.2 %copy-start.28 = (f32[512]{0:T(512)S(1)}, f32[512]{0:T(512)}, u32[]{:S(2)}) copy-start(f32[512]{0:T(512)} %copy-done.27) | copy-start | bytes 6148
  580.2 36.2 %copy-start.30 = (f32[1024]{0:T(1024)S(1)}, f32[1024]{0:T(1024)}, u32[]{:S(2)}) copy-start(f32[1024]{0:T(1024)} %param.16) | copy-start | bytes 12292
  635.7 80.8 %reduce-scatter.14.cloned.1.call-start = ((), (), s32[]{:S(2)}) async-start(), calls=%async_computation.15 | async-start | bytes 983040 | tf_op jit(solution)/shard_map/reduce_scatter | solution.py:518
  642.7 1.2 collective-permute-start.12
  643.9 4.4 collective-permute-start.13
  648.3 5.0 collective-permute-start.14
  653.3 39.8 %copy-start.26 = (f32[512]{0:T(512)S(1)}, f32[512]{0:T(512)}, u32[]{:S(2)}) copy-start(f32[512]{0:T(512)} %copy-done.25) | copy-start | bytes 6148
  653.3 42.3 %copy-start.7 = (f32[512,1024]{1,0:T(8,128)S(1)}, f32[512,1024]{1,0:T(8,128)}, u32[]{:S(2)}) copy-start(f32[512,1024]{1,0:T(8,128)} %copy-done.5) | copy-start | bytes 6291460
  653.3 39.8 %collective-permute-start.15 = (f32[17,128]{1,0:T(8,128)S(1)}, f32[17,128]{1,0:T(8,128)S(1)}, u32[]{:S(2)}, u32[]{:S(2)}) collective-permute-start(f32[17,128]{1,0:T(8,128)S(1)} %add.152), channel_id=1, source_target_pairs={{0,1},{1,0},{2,3},{3,2},{4,5},{5,4},{6,7},{7,6},{8,9},{9,8},{10,11... | collective-permute-start | bytes 26120 | tf_op jit(solution)/shard_map/ppermute | solution.py:529
  693.1 6.0 collective-permute-start.16
  (31 other events, 149.1 us)
Sparse Core Ops, SparseCore 0:
  30.6 36.0 all-gather.5
  69.2 38.5 all-gather.7
  110.3 43.5 all-gather.9
  155.7 40.2 all-gather.11
  449.8 47.6 reduce-scatter.15
  501.0 41.3 reduce-scatter.11
  545.9 66.5 reduce-scatter.9
  635.8 50.7 reduce-scatter.17
  693.2 23.2 reduce-scatter.13
